TPU v7x, 256 devices: a whole 4x4x8 slice. The times are simulated.
256 devices in a mesh: tm: 8 (over z_lo, y), head: 32 (over x, z_hi, core).
Axes of the slice: x: 4, y: 4, z: 8 (z_hi: 4, z_lo: 2; z = z_hi * 2 + z_lo), core: 2. Of those that a mesh axis runs over, the one named last changes fastest.
Arguments:
- queries: bfloat16 [32768, 2048], P(('tm', 'head')), may hold values from -16 to 16
- key_rows: bfloat16 [32768, 2048], P(('tm', 'head')), may hold values from -16 to 16
- value_rows: bfloat16 [32768, 2048], P(('tm', 'head')), may hold values from -16 to 16
- grad_out: bfloat16 [32768, 2048], P(('tm', 'head')), may hold values from -16 to 16
- windows: int32 [128, 6], replicated, may hold values from -1 to 127, as said below
- tile_place: int32 [16, 8], replicated, may hold values from 0 to 7, each once within a row
Outputs:
- out: bfloat16 [32768, 2048], P(('tm', 'head'))
- dq: bfloat16 [32768, 2048], P(('tm', 'head'))
- dk: bfloat16 [32768, 2048], P(('tm', 'head'))
- dv: bfloat16 [32768, 2048], P(('tm', 'head'))
Inputs may be any that keep to these rules, and one draw needn't show every extreme that they name: `windows`: row n lists the key tiles of natural tile n = 8 * t + 2 * y + x. Slots 2 * j and 2 * j + 1 hold a block of 2 tile rows by 1 tile column of time slice t - 1 + j that contains tile row y and column x, or -1 in both where that slice lies outside 0 to 15; tile n itself is always listed. `tile_place`: each row is a permutation of 0 to 7.
All inputs are finite; a program needn't handle non-finite values.
Results may differ from a plain program's by a relative error of at most 0.025.
Values may be sent and summed in bfloat16 or wider, within the bound.
A program may use at most 128 MiB of HBM per device.

v0:
```python
import jax
import jax.numpy as jnp
from jax import lax
from jax.sharding import PartitionSpec as P

HD = 128
HEADS = 16
TILE = 256
SH = 4
SW = 2
W = 6


def padded(array, sides, width):
    for axis, dim in sides:
        size, length = (lax.axis_size(axis), array.shape[dim])
        up = [(i, (i + 1) % size) for i in range(size - 1)]
        down = [(j, i) for i, j in up]
        last = lax.slice_in_dim(array, length - width, length, axis=dim)
        initial = lax.slice_in_dim(array, 0, width, axis=dim)
        before = lax.ppermute(last, axis, up)
        after = lax.ppermute(initial, axis, down)
        array = jnp.concatenate([before, array, after], axis=dim)
    return array


def from_behind(block, axis, distance):
    devices = range(lax.axis_size(axis))
    route = [(i - distance, i) for i in devices if i - distance in devices]
    return lax.ppermute(block, axis, route)


def pick_block(total_units, unit_rows):
    best_count = 1
    for trial_size in range(1, total_units + 1):
        if total_units % trial_size == 0 and trial_size * unit_rows <= max(512, unit_rows):
            best_count = trial_size
    return best_count


def body(queries, key_rows, value_rows, grad_out, windows, tile_place):
    tok_dev = queries.shape[0]
    head_dim = HD
    head_count = HEADS
    spatial = SH * SW
    tile_rows = TILE
    head_size = lax.axis_size("head")
    copies = head_size // head_count
    part_rows = tok_dev // copies
    group_tiles = tok_dev * head_size // tile_rows
    slices_group = group_tiles // spatial
    group_rows = tok_dev * head_size
    group_index = lax.axis_index("tm")
    my_part = lax.axis_index("head") % copies
    logit_scale = head_dim ** (-0.5)

    def split_parts(tensor):
        shaped = tensor.reshape(copies, part_rows, head_count, head_dim)
        return jnp.transpose(shaped, (1, 2, 0, 3)).reshape(part_rows, head_size, head_dim)

    def copy_parts(tensor):
        shaped = tensor.reshape(tok_dev, head_count, 1, head_dim)
        return jnp.broadcast_to(shaped, (tok_dev, head_count, copies, head_dim)).reshape(
            tok_dev, head_size, head_dim
        )

    def to_tokens(tensor):
        shaped = tensor.reshape(part_rows, head_count, copies, head_dim)
        return jnp.transpose(shaped, (2, 0, 1, 3)).reshape(tok_dev, head_count * head_dim)

    key_send, value_send = (copy_parts(key_rows), copy_parts(value_rows))
    head_queries, head_grads, head_keys, head_values = (
        lax.all_to_all(split_parts(queries), "head", split_axis=1, concat_axis=0, tiled=True),
        lax.all_to_all(split_parts(grad_out), "head", split_axis=1, concat_axis=0, tiled=True),
        lax.all_to_all(key_send, "head", split_axis=1, concat_axis=0, tiled=True),
        lax.all_to_all(value_send, "head", split_axis=1, concat_axis=0, tiled=True),
    )
    query_rows = head_queries.reshape(head_size * part_rows, head_dim)
    grad_rows = head_grads.reshape(head_size * part_rows, head_dim)
    group_keys = head_keys.reshape(group_rows, head_dim)
    group_values = head_values.reshape(group_rows, head_dim)
    slice_place = lax.dynamic_slice_in_dim(tile_place, group_index * slices_group, slices_group, 0)
    natural = (jnp.arange(slices_group, dtype=jnp.int32)[:, None] * spatial + slice_place).reshape(
        group_tiles
    )
    inverse = (
        jnp.zeros((group_tiles,), jnp.int32)
        .at[natural]
        .set(jnp.arange(group_tiles, dtype=jnp.int32))
    )
    key_tiles = group_keys.reshape(group_tiles, tile_rows, head_dim)[inverse]
    value_tiles = group_values.reshape(group_tiles, tile_rows, head_dim)[inverse]
    keys_ext, values_ext = (
        padded(key_tiles, (("tm", 0),), spatial),
        padded(value_tiles, (("tm", 0),), spatial),
    )
    unit_rows = min(tile_rows, part_rows)
    per_sender = part_rows // unit_rows
    unit_count = head_size * per_sender
    sender_ids = jnp.arange(unit_count, dtype=jnp.int32) // per_sender
    within_ids = jnp.arange(unit_count, dtype=jnp.int32) % per_sender
    local_rows = my_part * part_rows + within_ids * unit_rows
    stored_tile = (sender_ids * tok_dev + local_rows) // tile_rows
    unit_tile = natural[stored_tile] + group_index * group_tiles
    listed = windows[unit_tile]
    usable = listed >= 0
    ext_index = jnp.where(usable, listed - (group_index * group_tiles - spatial), 0)
    block_units = pick_block(unit_count, unit_rows)
    steps_total = unit_count // block_units
    query_units = query_rows.reshape(steps_total, block_units, unit_rows, head_dim)
    grad_units = grad_rows.reshape(steps_total, block_units, unit_rows, head_dim)
    index_units = ext_index.reshape(steps_total, block_units, W)
    usable_units = usable.reshape(steps_total, block_units, W)
    ext_tiles = group_tiles + 2 * spatial
    zero_grads = jnp.zeros((ext_tiles, tile_rows, head_dim), jnp.float32)

    def one_block(totals, pieces):
        total_keys, total_values = totals
        query_block_rows, gradient_block_rows, index_block, usable_block = pieces
        key_block_rows = keys_ext[index_block].reshape(block_units, W * tile_rows, head_dim)
        value_block_rows = values_ext[index_block].reshape(block_units, W * tile_rows, head_dim)
        key_mask = jnp.repeat(usable_block, tile_rows, axis=1)[:, None, :]
        logit_matrix = (
            jnp.einsum(
                "ast,ait->asi", query_block_rows, key_block_rows, preferred_element_type=jnp.float32
            )
            * logit_scale
        )
        logit_matrix = jnp.where(key_mask, logit_matrix, -jnp.inf)
        row_peak = jnp.max(logit_matrix, axis=2, keepdims=True)
        raised = jnp.exp(logit_matrix - row_peak)
        soft_weights = raised / jnp.sum(raised, axis=2, keepdims=True)
        weight_narrow = soft_weights.astype(jnp.bfloat16)
        output_block = jnp.einsum(
            "aiw,awu->aiu", weight_narrow, value_block_rows, preferred_element_type=jnp.float32
        ).astype(jnp.bfloat16)
        row_term = jnp.sum(
            gradient_block_rows.astype(jnp.float32) * output_block.astype(jnp.float32),
            axis=2,
            keepdims=True,
        )
        probability_gradient = jnp.einsum(
            "ast,ait->asi",
            gradient_block_rows,
            value_block_rows,
            preferred_element_type=jnp.float32,
        )
        score_gradient_narrow = (soft_weights * (probability_gradient - row_term)).astype(
            jnp.bfloat16
        )
        query_gradient_block = (
            jnp.einsum(
                "aiw,awu->aiu",
                score_gradient_narrow,
                key_block_rows,
                preferred_element_type=jnp.float32,
            )
            * logit_scale
        ).astype(jnp.bfloat16)
        key_gradient_terms = (
            jnp.einsum(
                "iuy,iuh->iyh",
                score_gradient_narrow,
                query_block_rows,
                preferred_element_type=jnp.float32,
            )
            * logit_scale
        )
        value_gradient_terms = jnp.einsum(
            "iuy,iuh->iyh", weight_narrow, gradient_block_rows, preferred_element_type=jnp.float32
        )
        flat_index = index_block.reshape(block_units * W)
        total_keys = total_keys.at[flat_index].add(
            key_gradient_terms.reshape(block_units * W, tile_rows, head_dim)
        )
        total_values = total_values.at[flat_index].add(
            value_gradient_terms.reshape(block_units * W, tile_rows, head_dim)
        )
        return ((total_keys, total_values), (output_block, query_gradient_block))

    (total_keys, total_values), (out_units, dq_units) = lax.scan(
        one_block, (zero_grads, zero_grads), (query_units, grad_units, index_units, usable_units)
    )
    next_keys, next_values = (
        from_behind(total_keys[:spatial].astype(jnp.bfloat16), "tm", -1).astype(jnp.float32),
        from_behind(total_values[:spatial].astype(jnp.bfloat16), "tm", -1).astype(jnp.float32),
    )
    prev_keys, prev_values = (
        from_behind(total_keys[spatial + group_tiles :].astype(jnp.bfloat16), "tm", 1).astype(
            jnp.float32
        ),
        from_behind(total_values[spatial + group_tiles :].astype(jnp.bfloat16), "tm", 1).astype(
            jnp.float32
        ),
    )
    grad_keys = total_keys[spatial : spatial + group_tiles]
    grad_values = total_values[spatial : spatial + group_tiles]
    grad_keys = grad_keys.at[group_tiles - spatial :].add(next_keys).at[:spatial].add(prev_keys)
    grad_values = (
        grad_values.at[group_tiles - spatial :].add(next_values).at[:spatial].add(prev_values)
    )
    stored_keys = grad_keys[natural].reshape(head_size, copies, part_rows, head_dim)
    stored_values = grad_values[natural].reshape(head_size, copies, part_rows, head_dim)
    back_out, back_dq = (
        lax.all_to_all(
            out_units.reshape(head_size, part_rows, 1, head_dim),
            "head",
            split_axis=0,
            concat_axis=2,
            tiled=True,
        ),
        lax.all_to_all(
            dq_units.reshape(head_size, part_rows, 1, head_dim),
            "head",
            split_axis=0,
            concat_axis=2,
            tiled=True,
        ),
    )
    send_keys = stored_keys.reshape(head_size, tok_dev, 1, head_dim)
    send_values = stored_values.reshape(head_size, tok_dev, 1, head_dim)
    back_keys, back_values = (
        lax.all_to_all(send_keys, "head", split_axis=0, concat_axis=2, tiled=True),
        lax.all_to_all(send_values, "head", split_axis=0, concat_axis=2, tiled=True),
    )
    dk_tokens = (
        back_keys.reshape(tok_dev, head_count, copies, head_dim)
        .sum(axis=2)
        .reshape(tok_dev, head_count * head_dim)
    )
    dv_tokens = (
        back_values.reshape(tok_dev, head_count, copies, head_dim)
        .sum(axis=2)
        .reshape(tok_dev, head_count * head_dim)
    )
    return (
        to_tokens(back_out),
        to_tokens(back_dq),
        dk_tokens.astype(jnp.bfloat16),
        dv_tokens.astype(jnp.bfloat16),
    )


def solution(mesh):
    in_specs = (
        P(("tm", "head"), None),
        P(("tm", "head"), None),
        P(("tm", "head"), None),
        P(("tm", "head"), None),
        P(),
        P(),
    )
    out_specs = (
        P(("tm", "head"), None),
        P(("tm", "head"), None),
        P(("tm", "head"), None),
        P(("tm", "head"), None),
    )
    return jax.shard_map(body, mesh=mesh, in_specs=in_specs, out_specs=out_specs, check_vma=False)
```

profile of v0, /device:TPU:35, one launch (start us, length us, event | category | flops | bytes accessed | tf_op | source)
XLA Modules:
  0.0 591.2 jit_solution(4122448184437392925)
XLA Ops:
  3.0 11.2 %all-to-all-start.1 = ((bf16[128,32,128]{2,0,1:T(8,128)(2,1)}), bf16[128,32,128]{2,0,1:T(8,128)(2,1)S(1)}, u32[]{:S(2)}, u32[]{:S(2)}) async-start(bf16[128,32,128]{2,0,1:T(8,128)(2,1)} %bitcast.22), calls=%async_computation.1 | async-start | bytes 2097152 | tf_op jit(solution)/shard_map/all_to_all | solution.py:75
  14.4 28.6 %all-to-all-done.1 = bf16[128,32,128]{2,0,1:T(8,128)(2,1)S(1)} async-done(((bf16[128,32,128]{2,0,1:T(8,128)(2,1)}), bf16[128,32,128]{2,0,1:T(8,128)(2,1)S(1)}, u32[]{:S(2)}, u32[]{:S(2)}) %all-to-all-start.1) | async-done | bytes 1048608 | tf_op jit(solution)/shard_map/all_to_all | solution.py:75
  54.5 18.2 %all-to-all-done.3 = bf16[128,32,128]{2,0,1:T(8,128)(2,1)S(1)} async-done(((bf16[128,32,128]{2,0,1:T(8,128)(2,1)}), bf16[128,32,128]{2,0,1:T(8,128)(2,1)S(1)}, u32[]{:S(2)}, u32[]{:S(2)}) %all-to-all-start.3) | async-done | bytes 1048608 | tf_op jit(solution)/shard_map/all_to_all | solution.py:76
  73.7 10.4 %all-to-all-start = ((bf16[64,32,128]{2,0,1:T(8,128)(2,1)}), bf16[64,32,128]{2,0,1:T(8,128)(2,1)S(1)}, u32[]{:S(2)}, u32[]{:S(2)}) async-start(bf16[64,32,128]{2,0,1:T(8,128)(2,1)} %bitcast.18), calls=%async_computation | async-start | bytes 1048576 | tf_op jit(solution)/shard_map/all_to_all | solution.py:73
  99.9 7.4 %all-to-all-start.2 = ((bf16[64,32,128]{2,0,1:T(8,128)(2,1)}), bf16[64,32,128]{2,0,1:T(8,128)(2,1)S(1)}, u32[]{:S(2)}, u32[]{:S(2)}) async-start(bf16[64,32,128]{2,0,1:T(8,128)(2,1)} %bitcast.28), calls=%async_computation.2 | async-start | bytes 1048576 | tf_op jit(solution)/shard_map/all_to_all | solution.py:74
  111.1 5.0 collective-permute-start.1
  119.0 15.6 %collective-permute-done = bf16[8,256,128]{2,1,0:T(8,128)(2,1)} collective-permute-done((bf16[8,256,128]{2,1,0:T(8,128)(2,1)}, bf16[8,256,128]{2,1,0:T(8,128)(2,1)}, u32[]{:S(2)}, u32[]{:S(2)}) %collective-permute-start) | collective-permute-done | bytes 524320 | tf_op jit(solution)/shard_map/ppermute | solution.py:21
  142.5 272.2 %while.20 = (s32[]{:T(128)}, f32[32,256,128]{2,1,0:T(8,128)}, f32[32,256,128]{2,1,0:T(8,128)}, bf16[4,8,64,128]{3,2,1,0:T(8,128)(2,1)}, bf16[4,8,64,128]{3,2,1,0...) while((s32[]{:T(128)}, f32[32,256,128]{2,1,0:T(8,128)}, ...), condition=%wide.region_7.8_spmd, body=%wide.region_1.7_spmd.sunk | while | flops 1224153344 | bytes 127578032 | solution.py:181
  154.2 5.1 fusion.85
  170.4 7.5 %fusion.87 = f32[8,1536,128]{2,1,0:T(8,128)} fusion(bf16[4,8,64,128]{3,2,1,0:T(8,128)(2,1)} %copy-done.11, s32[]{:T(128)S(6)} %copy.98, f32[8,64]{1,0:T(8,128)S(1)} %get-tuple-element.288, f32[8,64,1536]{2,1,0:T(8,128)} %fusion.84), kind=kOutput, calls=%fused_computation.29.clone.1 | convolution fusion | flops 203687936 | bytes 12716036 | tf_op jit(solution)/shard_map/while/body/eval_jaxpr/iuy,iuh->iyh/dot_general | solution.py:169
  177.9 14.4 %scatter_fusion.1 = f32[32,256,128]{2,1,0:T(8,128)} fusion(f32[32,256,128]{2,1,0:T(8,128)} %get-tuple-element.306, s32[48]{0:T(128)S(1)} %fusion.83, f32[48,256,128]{2,1,0:T(8,128)} %bitcast.191), kind=kCustom, calls=%fused_computation.9.clone.1 | custom fusion | flops 1572864 | bytes 18874560 | tf_op jit(solution)/shard_map/while/body/eval_jaxpr/scatter-add | solution.py:176
  196.1 14.3 %scatter_fusion = f32[32,256,128]{2,1,0:T(8,128)} fusion(f32[32,256,128]{2,1,0:T(8,128)} %get-tuple-element.305, s32[48]{0:T(128)S(1)} %fusion.83, f32[48,256,128]{2,1,0:T(8,128)} %bitcast.190), kind=kCustom, calls=%fused_computation.8.clone.1 | custom fusion | flops 1572864 | bytes 18874560 | tf_op jit(solution)/shard_map/while/body/eval_jaxpr/scatter-add | solution.py:173
  222.2 5.1 fusion.85
  227.3 5.0 multiply_reduce_fusion.2
  238.4 7.5 %fusion.87 = f32[8,1536,128]{2,1,0:T(8,128)} fusion(bf16[4,8,64,128]{3,2,1,0:T(8,128)(2,1)} %copy-done.11, s32[]{:T(128)S(6)} %copy.98, f32[8,64]{1,0:T(8,128)S(1)} %get-tuple-element.288, f32[8,64,1536]{2,1,0:T(8,128)} %fusion.84), kind=kOutput, calls=%fused_computation.29.clone.1 | convolution fusion | flops 203687936 | bytes 12716036 | tf_op jit(solution)/shard_map/while/body/eval_jaxpr/iuy,iuh->iyh/dot_general | solution.py:169
  245.9 14.4 %scatter_fusion.1 = f32[32,256,128]{2,1,0:T(8,128)} fusion(f32[32,256,128]{2,1,0:T(8,128)} %get-tuple-element.306, s32[48]{0:T(128)S(1)} %fusion.83, f32[48,256,128]{2,1,0:T(8,128)} %bitcast.191), kind=kCustom, calls=%fused_computation.9.clone.1 | custom fusion | flops 1572864 | bytes 18874560 | tf_op jit(solution)/shard_map/while/body/eval_jaxpr/scatter-add | solution.py:176
  264.0 14.3 %scatter_fusion = f32[32,256,128]{2,1,0:T(8,128)} fusion(f32[32,256,128]{2,1,0:T(8,128)} %get-tuple-element.305, s32[48]{0:T(128)S(1)} %fusion.83, f32[48,256,128]{2,1,0:T(8,128)} %bitcast.190), kind=kCustom, calls=%fused_computation.8.clone.1 | custom fusion | flops 1572864 | bytes 18874560 | tf_op jit(solution)/shard_map/while/body/eval_jaxpr/scatter-add | solution.py:173
  290.1 5.1 fusion.85
  306.3 7.5 %fusion.87 = f32[8,1536,128]{2,1,0:T(8,128)} fusion(bf16[4,8,64,128]{3,2,1,0:T(8,128)(2,1)} %copy-done.11, s32[]{:T(128)S(6)} %copy.98, f32[8,64]{1,0:T(8,128)S(1)} %get-tuple-element.288, f32[8,64,1536]{2,1,0:T(8,128)} %fusion.84), kind=kOutput, calls=%fused_computation.29.clone.1 | convolution fusion | flops 203687936 | bytes 12716036 | tf_op jit(solution)/shard_map/while/body/eval_jaxpr/iuy,iuh->iyh/dot_general | solution.py:169
  313.8 14.4 %scatter_fusion.1 = f32[32,256,128]{2,1,0:T(8,128)} fusion(f32[32,256,128]{2,1,0:T(8,128)} %get-tuple-element.306, s32[48]{0:T(128)S(1)} %fusion.83, f32[48,256,128]{2,1,0:T(8,128)} %bitcast.191), kind=kCustom, calls=%fused_computation.9.clone.1 | custom fusion | flops 1572864 | bytes 18874560 | tf_op jit(solution)/shard_map/while/body/eval_jaxpr/scatter-add | solution.py:176
  332.0 14.4 %scatter_fusion = f32[32,256,128]{2,1,0:T(8,128)} fusion(f32[32,256,128]{2,1,0:T(8,128)} %get-tuple-element.305, s32[48]{0:T(128)S(1)} %fusion.83, f32[48,256,128]{2,1,0:T(8,128)} %bitcast.190), kind=kCustom, calls=%fused_computation.8.clone.1 | custom fusion | flops 1572864 | bytes 18874560 | tf_op jit(solution)/shard_map/while/body/eval_jaxpr/scatter-add | solution.py:173
  358.2 5.1 fusion.85
  374.4 7.5 %fusion.87 = f32[8,1536,128]{2,1,0:T(8,128)} fusion(bf16[4,8,64,128]{3,2,1,0:T(8,128)(2,1)} %copy-done.11, s32[]{:T(128)S(6)} %copy.98, f32[8,64]{1,0:T(8,128)S(1)} %get-tuple-element.288, f32[8,64,1536]{2,1,0:T(8,128)} %fusion.84), kind=kOutput, calls=%fused_computation.29.clone.1 | convolution fusion | flops 203687936 | bytes 12716036 | tf_op jit(solution)/shard_map/while/body/eval_jaxpr/iuy,iuh->iyh/dot_general | solution.py:169
  381.9 14.5 %scatter_fusion.1 = f32[32,256,128]{2,1,0:T(8,128)} fusion(f32[32,256,128]{2,1,0:T(8,128)} %get-tuple-element.306, s32[48]{0:T(128)S(1)} %fusion.83, f32[48,256,128]{2,1,0:T(8,128)} %bitcast.191), kind=kCustom, calls=%fused_computation.9.clone.1 | custom fusion | flops 1572864 | bytes 18874560 | tf_op jit(solution)/shard_map/while/body/eval_jaxpr/scatter-add | solution.py:176
  400.2 14.4 %scatter_fusion = f32[32,256,128]{2,1,0:T(8,128)} fusion(f32[32,256,128]{2,1,0:T(8,128)} %get-tuple-element.305, s32[48]{0:T(128)S(1)} %fusion.83, f32[48,256,128]{2,1,0:T(8,128)} %bitcast.190), kind=kCustom, calls=%fused_computation.8.clone.1 | custom fusion | flops 1572864 | bytes 18874560 | tf_op jit(solution)/shard_map/while/body/eval_jaxpr/scatter-add | solution.py:173
  414.6 8.8 %all-to-all-start.4 = ((bf16[32,64,1,128]{3,1,2,0:T(8,128)(2,1)}), bf16[32,64,1,128]{3,1,2,0:T(8,128)(2,1)S(1)}, u32[]{:S(2)}, u32[]{:S(2)}) async-start(bf16[32,64,1,128]{3,1,2,0:T(8,128)(2,1)} %bitcast.36), calls=%async_computation.4 | async-start | bytes 1048576 | tf_op jit(solution)/shard_map/all_to_all | solution.py:205
  431.8 7.1 %all-to-all-done.4 = bf16[32,64,1,128]{3,1,2,0:T(8,128)(2,1)S(1)} async-done(((bf16[32,64,1,128]{3,1,2,0:T(8,128)(2,1)}), bf16[32,64,1,128]{3,1,2,0:T(8,128)(2,1)S(1)}, u32[]{:S(2)}, u32[]{:S(2)}) %all-to-all-start.4) | async-done | bytes 524320 | tf_op jit(solution)/shard_map/all_to_all | solution.py:205
  449.0 18.3 %collective-permute-done.5 = bf16[8,256,128]{2,1,0:T(8,128)(2,1)S(1)} collective-permute-done((bf16[8,256,128]{2,1,0:T(8,128)(2,1)}, bf16[8,256,128]{2,1,0:T(8,128)(2,1)S(1)}, u32[]{:S(2)}, u32[]{:S(2)}) %collective-permute-start.5) | collective-permute-done | bytes 524320 | tf_op jit(solution)/shard_map/ppermute | solution.py:30
  469.6 10.4 %all-to-all-start.6 = ((f32[32,128,1,128]{3,1,2,0:T(8,128)}), f32[32,128,1,128]{3,1,2,0:T(8,128)}, u32[]{:S(2)}, u32[]{:S(2)}) async-start(f32[32,128,1,128]{3,1,2,0:T(8,128)} %bitcast.194), calls=%async_computation.6 | async-start | bytes 4194304 | tf_op jit(solution)/shard_map/all_to_all | solution.py:223
  488.3 42.7 %collective-permute-done.6 = bf16[8,256,128]{2,1,0:T(8,128)(2,1)S(1)} collective-permute-done((bf16[8,256,128]{2,1,0:T(8,128)(2,1)S(1)}, bf16[8,256,128]{2,1,0:T(8,128)(2,1)S(1)}, u32[]{:S(2)}, u32[]{:S(2)}) %collective-permute-start.6) | collective-permute-done | bytes 524320 | tf_op jit(solution)/shard_map/ppermute | solution.py:30
  533.5 15.7 %all-to-all-start.7 = ((f32[32,128,1,128]{3,1,2,0:T(8,128)}), f32[32,128,1,128]{3,1,2,0:T(8,128)S(1)}, u32[]{:S(2)}, u32[]{:S(2)}) async-start(f32[32,128,1,128]{3,1,2,0:T(8,128)} %bitcast.195), calls=%async_computation.7 | async-start | bytes 4194304 | tf_op jit(solution)/shard_map/all_to_all | solution.py:224
  556.2 33.5 %all-to-all-done.7 = f32[32,128,1,128]{3,1,2,0:T(8,128)S(1)} async-done(((f32[32,128,1,128]{3,1,2,0:T(8,128)}), f32[32,128,1,128]{3,1,2,0:T(8,128)S(1)}, u32[]{:S(2)}, u32[]{:S(2)}) %all-to-all-start.7) | async-done | bytes 2097184 | tf_op jit(solution)/shard_map/all_to_all | solution.py:224
  (221 shorter events, 186.5 us)
Async XLA Ops:
  3.0 46.1 %copy-start.14 = (s32[16,8]{0,1:T(8,128)S(1)}, s32[16,8]{0,1:T(8,128)}, u32[]{:S(2)}) copy-start(s32[16,8]{0,1:T(8,128)} %param.21) | copy-start | bytes 1540
  3.0 46.4 %copy-start.13 = (s32[128,6]{0,1:T(8,128)S(1)}, s32[128,6]{0,1:T(8,128)}, u32[]{:S(2)}) copy-start(s32[128,6]{0,1:T(8,128)} %param.20) | copy-start | bytes 9220
  3.0 39.9 %all-to-all-start.1 = ((bf16[128,32,128]{2,0,1:T(8,128)(2,1)}), bf16[128,32,128]{2,0,1:T(8,128)(2,1)S(1)}, u32[]{:S(2)}, u32[]{:S(2)}) async-start(bf16[128,32,128]{2,0,1:T(8,128)(2,1)} %bitcast.22), calls=%async_computation.1 | async-start | bytes 2097152 | tf_op jit(solution)/shard_map/all_to_all | solution.py:75
  44.2 28.5 %all-to-all-start.3 = ((bf16[128,32,128]{2,0,1:T(8,128)(2,1)}), bf16[128,32,128]{2,0,1:T(8,128)(2,1)S(1)}, u32[]{:S(2)}, u32[]{:S(2)}) async-start(bf16[128,32,128]{2,0,1:T(8,128)(2,1)} %bitcast.32), calls=%async_computation.3 | async-start | bytes 2097152 | tf_op jit(solution)/shard_map/all_to_all | solution.py:76
  53.9 19.9 %copy-start.15 = (s32[16]{0:T(128)}, s32[16]{0:T(128)S(1)}, u32[]{:S(2)}) copy-start(s32[16]{0:T(128)S(1)} %fusion.30) | copy-start | bytes 196
  73.7 26.2 %all-to-all-start = ((bf16[64,32,128]{2,0,1:T(8,128)(2,1)}), bf16[64,32,128]{2,0,1:T(8,128)(2,1)S(1)}, u32[]{:S(2)}, u32[]{:S(2)}) async-start(bf16[64,32,128]{2,0,1:T(8,128)(2,1)} %bitcast.18), calls=%async_computation | async-start | bytes 1048576 | tf_op jit(solution)/shard_map/all_to_all | solution.py:73
  89.2 27.0 %collective-permute-start.2 = (bf16[8,256,128]{2,1,0:T(8,128)(2,1)}, bf16[8,256,128]{2,1,0:T(8,128)(2,1)}, u32[]{:S(2)}, u32[]{:S(2)}) collective-permute-start(bf16[8,256,128]{2,1,0:T(8,128)(2,1)} %get-tuple-element.207), channel_id=1, source_target_pairs={{0,32},{32,64},{64,96},{96,128},{128,160},{160,192},{192,224},{1,3... | collective-permute-start | bytes 1572872 | tf_op jit(solution)/shard_map/ppermute | solution.py:21
  92.4 23.8 %collective-permute-start.3 = (bf16[8,256,128]{2,1,0:T(8,128)(2,1)}, bf16[8,256,128]{2,1,0:T(8,128)(2,1)}, u32[]{:S(2)}, u32[]{:S(2)}) collective-permute-start(bf16[8,256,128]{2,1,0:T(8,128)(2,1)} %get-tuple-element.208), channel_id=1, source_target_pairs={{32,0},{64,32},{96,64},{128,96},{160,128},{192,160},{224,192},{33,... | collective-permute-start | bytes 1572872 | tf_op jit(solution)/shard_map/ppermute | solution.py:22
  99.9 37.5 %all-to-all-start.2 = ((bf16[64,32,128]{2,0,1:T(8,128)(2,1)}), bf16[64,32,128]{2,0,1:T(8,128)(2,1)S(1)}, u32[]{:S(2)}, u32[]{:S(2)}) async-start(bf16[64,32,128]{2,0,1:T(8,128)(2,1)} %bitcast.28), calls=%async_computation.2 | async-start | bytes 1048576 | tf_op jit(solution)/shard_map/all_to_all | solution.py:74
  108.3 26.2 %collective-permute-start = (bf16[8,256,128]{2,1,0:T(8,128)(2,1)}, bf16[8,256,128]{2,1,0:T(8,128)(2,1)}, u32[]{:S(2)}, u32[]{:S(2)}) collective-permute-start(bf16[8,256,128]{2,1,0:T(8,128)(2,1)} %get-tuple-element.209), channel_id=1, source_target_pairs={{0,32},{32,64},{64,96},{96,128},{128,160},{160,192},{192,224},{1,3... | collective-permute-start | bytes 1572872 | tf_op jit(solution)/shard_map/ppermute | solution.py:21
  111.1 23.4 %collective-permute-start.1 = (bf16[8,256,128]{2,1,0:T(8,128)(2,1)}, bf16[8,256,128]{2,1,0:T(8,128)(2,1)}, u32[]{:S(2)}, u32[]{:S(2)}) collective-permute-start(bf16[8,256,128]{2,1,0:T(8,128)(2,1)} %get-tuple-element.210), channel_id=1, source_target_pairs={{32,0},{64,32},{96,64},{128,96},{160,128},{192,160},{224,192},{33,... | collective-permute-start | bytes 1572872 | tf_op jit(solution)/shard_map/ppermute | solution.py:22
  177.9 14.4 %copy-start.4 = (bf16[8,64,1536]{2,1,0:T(8,128)(2,1)S(1)}, bf16[8,64,1536]{2,1,0:T(8,128)(2,1)}, u32[]{:S(2)}) copy-start(bf16[8,64,1536]{2,1,0:T(8,128)(2,1)} %copy-done.3) | copy-start | bytes 4718596 | tf_op jit(solution)/shard_map/while
  177.9 14.4 %copy-start.6 = (bf16[4,8,64,128]{3,2,1,0:T(8,128)(2,1)S(1)}, bf16[4,8,64,128]{3,2,1,0:T(8,128)(2,1)}, u32[]{:S(2)}) copy-start(bf16[4,8,64,128]{3,2,1,0:T(8,128)(2,1)} %copy-done.5) | copy-start | bytes 1572868 | tf_op jit(solution)/shard_map/while
  245.9 14.4 %copy-start.4 = (bf16[8,64,1536]{2,1,0:T(8,128)(2,1)S(1)}, bf16[8,64,1536]{2,1,0:T(8,128)(2,1)}, u32[]{:S(2)}) copy-start(bf16[8,64,1536]{2,1,0:T(8,128)(2,1)} %copy-done.3) | copy-start | bytes 4718596 | tf_op jit(solution)/shard_map/while
  245.9 14.4 %copy-start.6 = (bf16[4,8,64,128]{3,2,1,0:T(8,128)(2,1)S(1)}, bf16[4,8,64,128]{3,2,1,0:T(8,128)(2,1)}, u32[]{:S(2)}) copy-start(bf16[4,8,64,128]{3,2,1,0:T(8,128)(2,1)} %copy-done.5) | copy-start | bytes 1572868 | tf_op jit(solution)/shard_map/while
  313.8 14.4 %copy-start.4 = (bf16[8,64,1536]{2,1,0:T(8,128)(2,1)S(1)}, bf16[8,64,1536]{2,1,0:T(8,128)(2,1)}, u32[]{:S(2)}) copy-start(bf16[8,64,1536]{2,1,0:T(8,128)(2,1)} %copy-done.3) | copy-start | bytes 4718596 | tf_op jit(solution)/shard_map/while
  313.8 14.4 %copy-start.6 = (bf16[4,8,64,128]{3,2,1,0:T(8,128)(2,1)S(1)}, bf16[4,8,64,128]{3,2,1,0:T(8,128)(2,1)}, u32[]{:S(2)}) copy-start(bf16[4,8,64,128]{3,2,1,0:T(8,128)(2,1)} %copy-done.5) | copy-start | bytes 1572868 | tf_op jit(solution)/shard_map/while
  332.0 14.4 %copy-start.12 = (bf16[4,8,64,128]{3,2,1,0:T(8,128)(2,1)S(1)}, bf16[4,8,64,128]{3,2,1,0:T(8,128)(2,1)}, u32[]{:S(2)}) copy-start(bf16[4,8,64,128]{3,2,1,0:T(8,128)(2,1)} %copy-done.11) | copy-start | bytes 1572868 | tf_op jit(solution)/shard_map/while
  381.9 14.6 %copy-start.4 = (bf16[8,64,1536]{2,1,0:T(8,128)(2,1)S(1)}, bf16[8,64,1536]{2,1,0:T(8,128)(2,1)}, u32[]{:S(2)}) copy-start(bf16[8,64,1536]{2,1,0:T(8,128)(2,1)} %copy-done.3) | copy-start | bytes 4718596 | tf_op jit(solution)/shard_map/while
  381.9 14.6 %copy-start.6 = (bf16[4,8,64,128]{3,2,1,0:T(8,128)(2,1)S(1)}, bf16[4,8,64,128]{3,2,1,0:T(8,128)(2,1)}, u32[]{:S(2)}) copy-start(bf16[4,8,64,128]{3,2,1,0:T(8,128)(2,1)} %copy-done.5) | copy-start | bytes 1572868 | tf_op jit(solution)/shard_map/while
  400.2 14.4 %copy-start.12 = (bf16[4,8,64,128]{3,2,1,0:T(8,128)(2,1)S(1)}, bf16[4,8,64,128]{3,2,1,0:T(8,128)(2,1)}, u32[]{:S(2)}) copy-start(bf16[4,8,64,128]{3,2,1,0:T(8,128)(2,1)} %copy-done.11) | copy-start | bytes 1572868 | tf_op jit(solution)/shard_map/while
  414.6 24.3 %all-to-all-start.4 = ((bf16[32,64,1,128]{3,1,2,0:T(8,128)(2,1)}), bf16[32,64,1,128]{3,1,2,0:T(8,128)(2,1)S(1)}, u32[]{:S(2)}, u32[]{:S(2)}) async-start(bf16[32,64,1,128]{3,1,2,0:T(8,128)(2,1)} %bitcast.36), calls=%async_computation.4 | async-start | bytes 1048576 | tf_op jit(solution)/shard_map/all_to_all | solution.py:205
  426.0 19.8 %copy-start.16 = (s32[16]{0:T(128)S(1)}, s32[16]{0:T(128)}, u32[]{:S(2)}) copy-start(s32[16]{0:T(128)} %copy-done.15) | copy-start | bytes 196
  427.0 20.5 %collective-permute-start.4 = (bf16[8,256,128]{2,1,0:T(8,128)(2,1)}, bf16[8,256,128]{2,1,0:T(8,128)(2,1)}, u32[]{:S(2)}, u32[]{:S(2)}) collective-permute-start(bf16[8,256,128]{2,1,0:T(8,128)(2,1)} %get-tuple-element.206), channel_id=1, source_target_pairs={{32,0},{64,32},{96,64},{128,96},{160,128},{192,160},{224,192},{33,... | collective-permute-start | bytes 1572872 | tf_op jit(solution)/shard_map/ppermute | solution.py:30
  438.9 30.7 %all-to-all-start.5 = ((bf16[32,64,1,128]{3,1,2,0:T(8,128)(2,1)}), bf16[32,64,1,128]{3,1,2,0:T(8,128)(2,1)S(1)}, u32[]{:S(2)}, u32[]{:S(2)}) async-start(bf16[32,64,1,128]{3,1,2,0:T(8,128)(2,1)} %bitcast.41), calls=%async_computation.5 | async-start | bytes 1048576 | tf_op jit(solution)/shard_map/all_to_all | solution.py:212
  443.8 23.5 %collective-permute-start.5 = (bf16[8,256,128]{2,1,0:T(8,128)(2,1)}, bf16[8,256,128]{2,1,0:T(8,128)(2,1)S(1)}, u32[]{:S(2)}, u32[]{:S(2)}) collective-permute-start(bf16[8,256,128]{2,1,0:T(8,128)(2,1)} %get-tuple-element.205), channel_id=1, source_target_pairs={{0,32},{32,64},{64,96},{96,128},{128,160},{160,192},{192,224},{1,3... | collective-permute-start | bytes 1572872 | tf_op jit(solution)/shard_map/ppermute | solution.py:30
  469.6 63.8 %all-to-all-start.6 = ((f32[32,128,1,128]{3,1,2,0:T(8,128)}), f32[32,128,1,128]{3,1,2,0:T(8,128)}, u32[]{:S(2)}, u32[]{:S(2)}) async-start(f32[32,128,1,128]{3,1,2,0:T(8,128)} %bitcast.194), calls=%async_computation.6 | async-start | bytes 4194304 | tf_op jit(solution)/shard_map/all_to_all | solution.py:223
  482.8 48.2 %collective-permute-start.6 = (bf16[8,256,128]{2,1,0:T(8,128)(2,1)S(1)}, bf16[8,256,128]{2,1,0:T(8,128)(2,1)S(1)}, u32[]{:S(2)}, u32[]{:S(2)}) collective-permute-start(bf16[8,256,128]{2,1,0:T(8,128)(2,1)S(1)} %get-tuple-element.204), channel_id=1, source_target_pairs={{32,0},{64,32},{96,64},{128,96},{160,128},{192,160},{224,192},{33,... | collective-permute-start | bytes 1572872 | tf_op jit(solution)/shard_map/ppermute | solution.py:30
  484.7 46.4 %collective-permute-start.7 = (bf16[8,256,128]{2,1,0:T(8,128)(2,1)S(1)}, bf16[8,256,128]{2,1,0:T(8,128)(2,1)S(1)}, u32[]{:S(2)}, u32[]{:S(2)}) collective-permute-start(bf16[8,256,128]{2,1,0:T(8,128)(2,1)S(1)} %get-tuple-element.203), channel_id=1, source_target_pairs={{0,32},{32,64},{64,96},{96,128},{128,160},{160,192},{192,224},{1,3... | collective-permute-start | bytes 1572872 | tf_op jit(solution)/shard_map/ppermute | solution.py:30
  533.5 16.1 %copy-start.9 = (bf16[32,64,1,128]{3,1,2,0:T(8,128)(2,1)S(1)}, bf16[32,64,1,128]{3,1,2,0:T(8,128)(2,1)}, u32[]{:S(2)}) copy-start(bf16[32,64,1,128]{3,1,2,0:T(8,128)(2,1)} %copy-done.8) | copy-start | bytes 1572868
  533.5 56.2 %all-to-all-start.7 = ((f32[32,128,1,128]{3,1,2,0:T(8,128)}), f32[32,128,1,128]{3,1,2,0:T(8,128)S(1)}, u32[]{:S(2)}, u32[]{:S(2)}) async-start(f32[32,128,1,128]{3,1,2,0:T(8,128)} %bitcast.195), calls=%async_computation.7 | async-start | bytes 4194304 | tf_op jit(solution)/shard_map/all_to_all | solution.py:224
  553.8 37.4 %copy-start.1 = (bf16[128,2048]{1,0:T(8,128)(2,1)S(1)}, bf16[128,2048]{1,0:T(8,128)(2,1)}, u32[]{:S(2)}) copy-start(bf16[128,2048]{1,0:T(8,128)(2,1)} %param.17) | copy-start | bytes 1572868
  (19 other events, 78.0 us)
where the time goes:
time: 596 us; the launch traced here: 591 us
  waiting for transfers between devices  167 us (28%)
  other arithmetic  151 us (25%)
  matrix products  102 us (17%)
  starting transfers between devices  101 us (17%)
  local copies, waits for them, and re-layouts  68.4 us (11%)
    ppermute x4, waiting for transfers between devices, from_behind(): return lax.ppermute(block, axis, route)  61.1 us
    scatter-add x4, other arithmetic, one_block(): total_values.at[flat_index]  57.7 us
    scatter-add x4, other arithmetic, one_block(): total_keys.at[flat_index]  57.4 us
    all_to_all x1, waiting for transfers between devices, body(): lax.all_to_all(send_values, 'head', split_axis=0, concat_axis=2, tiled=True)  33.5 us
    dot_general x4, matrix products, one_block(): jnp.einsum('iuy,iuh->iyh', weight_narrow, gradient_block_rows, preferred_...  30 us
    all_to_all x1, waiting for transfers between devices, body(): lax.all_to_all(key_send, 'head', split_axis=1, concat_axis=0, tiled=True)  28.6 us
    sub x4, other arithmetic, one_block(): raised = jnp.exp(logit_matrix - row_peak)  20.3 us
    dot_general x4, matrix products, one_block(): jnp.einsum('aiw,awu->aiu', weight_narrow, value_block_rows, preferred_ele...  19.9 us
  transfers between devices with their start and end apart: 16, of which 8 were waited for; matrix products, arithmetic and copies ran while one was open for 7% of the time, Pallas kernels for 0%

commit v1 on v0

v1 whole, which is shorter than its diff:
```python
import functools

import jax
import jax.numpy as jnp
import numpy as np
from jax import lax
from jax.sharding import PartitionSpec as P
import jax.experimental.pallas as pl
import jax.experimental.pallas.tpu as pltpu

HD = 128
HEADS = 16
TILE = 256
SP = 8
W = 6
HALF = 128
NONE = SP * W
MESH = pl.DeviceIdType.MESH
BF = jnp.bfloat16
F32 = jnp.float32
SCALE = HD**-0.5
SCALE2 = float(SCALE * np.log2(np.e))
NN = (((1,), (0,)), ((), ()))
TN = (((0,), (0,)), ((), ()))


def dot(a, b, dims):
    return lax.dot_general(a, b, dims, preferred_element_type=F32)


def place():
    group = lax.axis_index("tm")
    index = lax.axis_index("head")
    return group, index, index // HEADS, lax.rem(index, HEADS), index // 2, lax.rem(index, 2)


def around():
    group, index, _, _, _, core = place()
    other = index + 1 - 2 * core
    before = (group - 1 + core, other)
    after = (group + core, other)
    has_before = (core == 1) | (group > 0)
    has_after = (core == 0) | (group < lax.axis_size("tm") - 1)
    return before, after, has_before, has_after


def greet():
    group, index, half, _, _, core = place()
    barrier = pltpu.get_barrier_semaphore()

    def signal(i, carry):
        for other in (2 * i + half, HEADS * core + i):

            @pl.when(other != index)
            def _():
                pl.semaphore_signal(barrier, 1, device_id=(group, other), device_id_type=MESH)

        return carry

    lax.fori_loop(0, HEADS, signal, 0)
    before, after, has_before, has_after = around()

    @pl.when(has_before)
    def _():
        pl.semaphore_signal(barrier, 1, device_id=before, device_id_type=MESH)

    @pl.when(has_after)
    def _():
        pl.semaphore_signal(barrier, 1, device_id=after, device_id_type=MESH)

    own = jnp.where(half == core, 2, 0)
    pl.semaphore_wait(barrier, 2 * HEADS - own + has_before.astype(jnp.int32) + has_after.astype(jnp.int32))


def landed(ref, sem):
    pltpu.make_async_copy(ref, ref, sem).wait()


def send(src, dst, send_sem, recv_sem, target):
    pltpu.make_async_remote_copy(
        src_ref=src, dst_ref=dst, send_sem=send_sem, recv_sem=recv_sem, device_id=target, device_id_type=MESH
    ).start()


def half_rows(ref, i, first=0):
    return ref.at[first + i // 2, pl.ds(pl.multiple_of(lax.rem(i, 2) * HALF, HALF), HALF)]


def head_columns(ref, h):
    return ref.at[:, pl.ds(pl.multiple_of(h * HD, HD), HD)]


def loop(n, step):
    def body(i, carry):
        step(i)
        return carry

    lax.fori_loop(0, n, body, 0)


def gather_kernel(q_in, k_in, v_in, g_in, q, kx, vx, g, sent, got, halo_sent, halo_got):
    group, index, half, mine, head, core = place()
    greet()
    arrays = ((k_in, kx, SP), (v_in, vx, SP), (q_in, q, 0), (g_in, g, 0))
    for a, (src, dst, first) in enumerate(arrays):

        def push(n):
            h = lax.rem(head + n, HEADS)
            target = 2 * h + half

            @pl.when(target != index)
            def _():
                send(
                    head_columns(src, h),
                    half_rows(dst, mine, first),
                    sent.at[a, n],
                    got.at[a, mine],
                    (group, target),
                )

            @pl.when(target == index)
            def _():
                pltpu.make_async_copy(head_columns(src, h), half_rows(dst, mine, first), got.at[a, mine]).start()

        loop(HEADS, push)

    before, after, has_before, has_after = around()
    for a, (src, dst, first) in enumerate(arrays):
        loop(HEADS, lambda i: landed(half_rows(dst, i, first), got.at[a, i]))
        if a < 2:
            own = dst.at[pl.ds(SP, SP)]

            @pl.when(has_before)
            def _():
                send(own, dst.at[pl.ds(2 * SP, SP)], halo_sent.at[a, 0], halo_got.at[a, 1], before)

            @pl.when(has_after)
            def _():
                send(own, dst.at[pl.ds(0, SP)], halo_sent.at[a, 1], halo_got.at[a, 0], after)

    for a, dst in enumerate((kx, vx)):
        own = dst.at[pl.ds(SP, SP)]

        @pl.when(has_before)
        def _():
            landed(dst.at[pl.ds(0, SP)], halo_got.at[a, 0])
            landed(own, halo_sent.at[a, 0])

        @pl.when(has_after)
        def _():
            landed(dst.at[pl.ds(2 * SP, SP)], halo_got.at[a, 1])
            landed(own, halo_sent.at[a, 1])

    for a, (src, dst, first) in enumerate(arrays):

        def drain(n):
            h = lax.rem(head + n, HEADS)

            @pl.when(2 * h + half != index)
            def _():
                landed(half_rows(dst, mine, first), sent.at[a, n])

        loop(HEADS, drain)


def tables(windows, tile_place, inverse, key_at, usable, query_of, pair_of):
    group, _, _, _, _, core = place()
    slice_id = 2 * group + core
    last = 2 * lax.axis_size("tm") - 1

    def invert(n):
        near = jnp.clip(slice_id - 1 + n // SP, 0, last)
        tile = lax.rem(n, SP)
        found = jnp.int32(0)
        for i in range(SP):
            found = found + jnp.where(tile_place[near, i] == tile, i, 0)
        inverse[n] = found

    loop(3 * SP, invert)

    def query(n):
        i = n // W
        w = lax.rem(n, W)
        tile = SP * slice_id + tile_place[slice_id, i]
        listed = windows[tile, w]
        good = listed >= 0
        named = jnp.where(good, listed, windows[tile, 2])
        key_at[n] = inverse[named - SP * (slice_id - 1)] + SP * jnp.where(good, w // 2, 1)
        usable[n] = good.astype(jnp.int32)

    loop(SP * W, query)

    def key(n):
        m = n // 3
        j = m // SP
        near = jnp.clip(slice_id - 1 + j, 0, last)
        tile = tile_place[near, lax.rem(m, SP)]
        row = tile // 2 + lax.rem(n, 3) - 1
        inside = (row >= 0) & (row < SP // 2)
        asker = jnp.where(inside, 2 * row + lax.rem(tile, 2), 0)
        i = inverse[SP + asker]
        name = SP * near + tile
        first = windows[SP * slice_id + asker, 2 * j] == name
        second = windows[SP * slice_id + asker, 2 * j + 1] == name
        query_of[n] = i
        pair_of[n] = jnp.where(
            inside & (first | second), i * W + 2 * j + jnp.where(second, 1, 0), NONE
        )

    loop(9 * SP, key)


def query_tile(i, key_at, usable, q, g, kx, vx, o, dq, probs, dscores, q_scaled, g_scaled):
    q_rows = q[i]
    g_rows = g[i]
    q_turned = q_rows.T
    g_turned = g_rows.T
    at = [key_at[i * W + w] for w in range(W)]
    scores = [dot(kx[at[w]], q_turned, NN) for w in range(W)]
    peak = scores[0]
    for w in range(1, W):
        peak = jnp.maximum(peak, scores[w])
    peak = jnp.max(peak, axis=0, keepdims=True) * SCALE2
    total = jnp.zeros((1, TILE), F32)
    out = jnp.zeros((HD, TILE), F32)
    raised = []
    for w in range(W):
        level = peak + jnp.where(usable[i * W + w] > 0, 0.0, 1e30)
        e = jnp.exp2(scores[w] * SCALE2 - level)
        total = total + jnp.sum(e, axis=0, keepdims=True)
        low = e.astype(BF)
        probs[i * W + w] = low
        raised.append(e)
        out = out + dot(vx[at[w]], low, TN)
    share = 1.0 / total
    out_low = (out * share).astype(BF)
    o[i] = out_low.T
    row_term = jnp.sum(g_turned.astype(F32) * out_low.astype(F32), axis=0, keepdims=True)
    grad = jnp.zeros((HD, TILE), F32)
    for w in range(W):
        dprobs = dot(vx[at[w]], g_turned, NN)
        low = (raised[w] * (dprobs - row_term)).astype(BF)
        dscores[i * W + w] = low
        grad = grad + dot(kx[at[w]], low, TN)
    dq[i] = (grad * (share * SCALE)).astype(BF).T
    share_rows = jnp.transpose(jnp.broadcast_to(share, (HD, TILE)))
    q_scaled[i] = (q_rows.astype(F32) * (share_rows * SCALE)).astype(BF)
    g_scaled[i] = (g_rows.astype(F32) * share_rows).astype(BF)


def key_tile(m, query_of, pair_of, q_scaled, g_scaled, probs, dscores):
    grad_k = jnp.zeros((TILE, HD), F32)
    grad_v = jnp.zeros((TILE, HD), F32)
    for n in range(3):
        i = query_of[3 * m + n]
        pair = pair_of[3 * m + n]
        grad_v = grad_v + dot(probs[pair], g_scaled[i], NN)
        grad_k = grad_k + dot(dscores[pair], q_scaled[i], NN)
    return grad_k, grad_v


def compute_kernel(
    windows, tile_place, q, kx, vx, g, o, dq, dk, dv, dk_far, dv_far,
    inverse, key_at, usable, query_of, pair_of, probs, dscores, q_scaled, g_scaled,
):
    tables(windows, tile_place, inverse, key_at, usable, query_of, pair_of)
    probs[NONE] = jnp.zeros((TILE, TILE), BF)
    dscores[NONE] = jnp.zeros((TILE, TILE), BF)
    loop(SP, lambda i: query_tile(i, key_at, usable, q, g, kx, vx, o, dq, probs, dscores, q_scaled, g_scaled))

    def own(m):
        dk[m], dv[m] = key_tile(SP + m, query_of, pair_of, q_scaled, g_scaled, probs, dscores)

    def far(n):
        m = jnp.where(n < SP, n, n + SP)
        grad_k, grad_v = key_tile(m, query_of, pair_of, q_scaled, g_scaled, probs, dscores)
        dk_far[n] = grad_k.astype(BF)
        dv_far[n] = grad_v.astype(BF)

    loop(2 * SP, far)
    loop(SP, own)


def return_kernel(
    o, dq, dk, dv, dk_far, dv_far, o_out, dq_out, dk_out, dv_out,
    dk_near, dv_near, dk_low, dv_low, sent, got, halo_sent, halo_got,
):
    group, index, half, mine, head, core = place()
    greet()
    before, after, has_before, has_after = around()
    for a, (far, near) in enumerate(((dk_far, dk_near), (dv_far, dv_near))):

        @pl.when(has_before)
        def _():
            send(far.at[pl.ds(0, SP)], near.at[pl.ds(SP, SP)], halo_sent.at[a, 0], halo_got.at[a, 1], before)

        @pl.when(has_after)
        def _():
            send(far.at[pl.ds(SP, SP)], near.at[pl.ds(0, SP)], halo_sent.at[a, 1], halo_got.at[a, 0], after)

    def push_all(a, src, dst):
        def push(n):
            i = lax.rem(mine + n, HEADS)
            target = HEADS * core + i

            @pl.when(target != index)
            def _():
                send(half_rows(src, i), head_columns(dst, head), sent.at[a, n], got.at[a, head], (group, target))

            @pl.when(target == index)
            def _():
                pltpu.make_async_copy(half_rows(src, i), head_columns(dst, head), got.at[a, head]).start()

        loop(HEADS, push)

    push_all(0, o, o_out)
    push_all(1, dq, dq_out)

    sums = ((dk, dk_far, dk_near, dk_low, dk_out), (dv, dv_far, dv_near, dv_low, dv_out))
    for a, (full, far, near, low, out) in enumerate(sums):

        @pl.when(has_before)
        def _():
            landed(near.at[pl.ds(0, SP)], halo_got.at[a, 0])
            landed(far.at[pl.ds(0, SP)], halo_sent.at[a, 0])

        @pl.when(jnp.logical_not(has_before))
        def _():
            near[pl.ds(0, SP)] = jnp.zeros((SP, TILE, HD), BF)

        @pl.when(has_after)
        def _():
            landed(near.at[pl.ds(SP, SP)], halo_got.at[a, 1])
            landed(far.at[pl.ds(SP, SP)], halo_sent.at[a, 1])

        @pl.when(jnp.logical_not(has_after))
        def _():
            near[pl.ds(SP, SP)] = jnp.zeros((SP, TILE, HD), BF)

        def add(m):
            low[m] = (full[m] + near[m].astype(F32) + near[SP + m].astype(F32)).astype(BF)

        loop(SP, add)
        push_all(2 + a, low, out)

    for a, (src, dst) in enumerate(((o, o_out), (dq, dq_out), (dk_low, dk_out), (dv_low, dv_out))):

        def drain(n):
            landed(head_columns(dst, n), got.at[a, n])
            i = lax.rem(mine + n, HEADS)

            @pl.when(HEADS * core + i != index)
            def _():
                landed(half_rows(src, i), sent.at[a, n])

        loop(HEADS, drain)


def body(queries, key_rows, value_rows, grad_out, windows, tile_place):
    anywhere = pl.BlockSpec(memory_space=pl.ANY)
    vmem = pl.BlockSpec(memory_space=pltpu.VMEM)
    smem = pl.BlockSpec(memory_space=pltpu.SMEM)
    tiles = lambda n, kind=BF: jax.ShapeDtypeStruct((n, TILE, HD), kind)
    rows = jax.ShapeDtypeStruct(queries.shape, BF)
    dma = pltpu.SemaphoreType.DMA
    limit = 56 * 1024 * 1024

    q, kx, vx, g = pl.pallas_call(
        gather_kernel,
        out_shape=[tiles(SP), tiles(3 * SP), tiles(3 * SP), tiles(SP)],
        in_specs=[anywhere] * 4,
        out_specs=[vmem] * 4,
        scratch_shapes=[dma((4, HEADS)), dma((4, HEADS)), dma((2, 2)), dma((2, 2))],
        compiler_params=pltpu.CompilerParams(collective_id=0, has_side_effects=True, vmem_limit_bytes=limit),
        name="gather",
    )(queries, key_rows, value_rows, grad_out)

    o, dq, dk, dv, dk_far, dv_far = pl.pallas_call(
        compute_kernel,
        out_shape=[tiles(SP), tiles(SP), tiles(SP, F32), tiles(SP, F32), tiles(2 * SP), tiles(2 * SP)],
        in_specs=[smem] * 2 + [vmem] * 4,
        out_specs=[vmem] * 6,
        scratch_shapes=[
            pltpu.SMEM((3 * SP,), jnp.int32),
            pltpu.SMEM((SP * W,), jnp.int32),
            pltpu.SMEM((SP * W,), jnp.int32),
            pltpu.SMEM((9 * SP,), jnp.int32),
            pltpu.SMEM((9 * SP,), jnp.int32),
            pltpu.VMEM((NONE + 1, TILE, TILE), BF),
            pltpu.VMEM((NONE + 1, TILE, TILE), BF),
            pltpu.VMEM((SP, TILE, HD), BF),
            pltpu.VMEM((SP, TILE, HD), BF),
        ],
        compiler_params=pltpu.CompilerParams(vmem_limit_bytes=limit),
        name="compute",
    )(windows, tile_place, q, kx, vx, g)

    return pl.pallas_call(
        return_kernel,
        out_shape=[rows] * 4,
        in_specs=[vmem] * 6,
        out_specs=[anywhere] * 4,
        scratch_shapes=[
            pltpu.VMEM((2 * SP, TILE, HD), BF),
            pltpu.VMEM((2 * SP, TILE, HD), BF),
            pltpu.VMEM((SP, TILE, HD), BF),
            pltpu.VMEM((SP, TILE, HD), BF),
            dma((4, HEADS)),
            dma((4, HEADS)),
            dma((2, 2)),
            dma((2, 2)),
        ],
        compiler_params=pltpu.CompilerParams(collective_id=1, has_side_effects=True, vmem_limit_bytes=limit),
        name="send_back",
    )(o, dq, dk, dv, dk_far, dv_far)


def solution(mesh):
    spread = P(("tm", "head"), None)
    return jax.shard_map(
        body,
        mesh=mesh,
        in_specs=(spread,) * 4 + (P(), P()),
        out_specs=(spread,) * 4,
        check_vma=False,
    )
```

time: 596 us -> 173 us (0.29)
  waiting for transfers between devices: 167 us -> 0 us
  Pallas kernels: 0 us -> 161 us
  other arithmetic: 151 us -> 0 us
  matrix products: 102 us -> 0 us
  starting transfers between devices: 101 us -> 0 us
  local copies, waits for them, and re-layouts: 68.4 us -> 8.22 us
    pallas_call x0 -> x3, Pallas kernels: none -> 161 us  [the longest x1 71.2 us: body(): pl.pallas_call(return_kernel, out_shape=[rows] * 4, in_specs=[vmem] * 6,...]
    scatter-add x12 -> x0, other arithmetic: 117 us -> none  [the longest x4 57.7 us: one_block(): total_values.at[flat_index]]
    dot_general x24 -> x0, matrix products: 102 us -> none  [the longest x4 30 us: one_block(): jnp.einsum('iuy,iuh->iyh', weight_narrow, gradient_block_rows, preferred_...]
    all_to_all x8 -> x0, waiting for transfers between devices: 90.2 us -> none  [the longest x1 33.5 us: body(): lax.all_to_all(send_values, 'head', split_axis=0, concat_axis=2, tiled=True)]
    ppermute x8 -> x0, waiting for transfers between devices: 76.7 us -> none  [the longest x4 61.1 us: from_behind(): return lax.ppermute(block, axis, route)]
    all_to_all x8 -> x0, starting transfers between devices: 73.6 us -> none  [the longest x1 15.7 us: body(): lax.all_to_all(send_values, 'head', split_axis=0, concat_axis=2, tiled=True)]
    gather x14 -> x0, local copies, waits for them, and re-layouts: 36.1 us -> none  [the longest x4 17.2 us: one_block(): values_ext[index_block].reshape(block_units, W * tile_rows, head_dim)]
    ppermute x8 -> x0, starting transfers between devices: 27.7 us -> none  [the longest x4 12 us: from_behind(): return lax.ppermute(block, axis, route)]
  transfers between devices with their start and end apart: 16 -> 0, of which waited for: 8 -> 0; matrix products, arithmetic and copies ran while one was open for 7% -> 0% of each run, Pallas kernels for 0% -> 0%
where the time goes in v1:
time: 173 us; the launch traced here: 170 us
  Pallas kernels  161 us (93%)
  local copies, waits for them, and re-layouts  8.22 us (5%)
    pallas_call x1, Pallas kernels, body(): pl.pallas_call(return_kernel, out_shape=[rows] * 4, in_specs=[vmem] * 6,...  71.2 us
    pallas_call x1, Pallas kernels, body(): pl.pallas_call(gather_kernel, out_shape=[tiles(SP), tiles(3 * SP), tiles(...  57.8 us
    pallas_call x1, Pallas kernels, body(): pl.pallas_call(compute_kernel, out_shape=[tiles(SP), tiles(SP), tiles(SP,...  32 us
    unnamed x10, local copies, waits for them, and re-layouts  8.22 us

profile of v1, /device:TPU:35, one launch (start us, length us, event | category | flops | bytes accessed | tf_op | source)
XLA Modules:
  0.0 169.9 jit_solution(14665758278236854112)
XLA Ops:
  0.6 1.4 copy.11.tile_place
  2.0 1.4 copy.10.windows
  3.4 57.8 %gather.1 = (bf16[8,256,128]{2,1,0:T(8,128)(2,1)}, bf16[24,256,128]{2,1,0:T(8,128)(2,1)}, bf16[24,256,128]{2,1,0:T(8,128)(2,1)}, bf16[8,256,128]{2,1,0:T(8,128)(2,1)}) custom-call(bf16[128,2048]{1,0:T(8,128)(2,1)} %q_in.1, bf16[128,2048]{1,0:T(8,128)(2,1)} %k_in.1, bf16[128,2048]{1,0:T(8,128)(2,1)} %v_in.1, bf16[128,2048]{1,0:T(8,128)(2,1)} %g_in.1), custom_call_target="tpu_custom_call" | custom-call | tf_op jit(solution)/shard_map/gather/pallas_call | solution.py:368
  61.2 32.0 %compute.1 = (bf16[8,256,128]{2,1,0:T(8,128)(2,1)}, bf16[8,256,128]{2,1,0:T(8,128)(2,1)}, f32[8,256,128]{2,1,0:T(8,128)}, f32[8,256,128]{2,1,0:T(8,128)}, bf16[1...) custom-call(s32[128,6]{1,0:T(8,128)} %copy.10.windows, s32[16,8]{1,0:T(8,128)} %copy.11.tile_place, ...), custom_call_target="tpu_custom_call" | custom-call | tf_op jit(solution)/shard_map/compute/pallas_call | solution.py:378
  93.2 71.2 %send_back.1 = (bf16[128,2048]{1,0:T(8,128)(2,1)}, bf16[128,2048]{1,0:T(8,128)(2,1)}, bf16[128,2048]{1,0:T(8,128)(2,1)}, bf16[128,2048]{1,0:T(8,128)(2,1)}) custom-call(bf16[8,256,128]{2,1,0:T(8,128)(2,1)} %get-tuple-element.18.o, bf16[8,256,128]{2,1,0:T(8,128)(2,1)} %get-tuple-element.19.dq, f32[8,256,128]{2,1,0:T(8,128)} %get-tuple-element.20.dk, ...), custom_call_target="tpu_custom_call" | custom-call | tf_op jit(solution)/shard_map/send_back/pallas_call | solution.py:398
  164.4 0.0 copy-start.1
  164.5 0.0 copy-start
  164.5 2.0 %copy.16 = bf16[128,2048]{1,0:T(8,128)(2,1)} copy(bf16[128,2048]{1,0:T(8,128)(2,1)} %get-tuple-element.28) | data formatting | bytes 1048576
  166.4 1.9 %copy.17 = bf16[128,2048]{1,0:T(8,128)(2,1)} copy(bf16[128,2048]{1,0:T(8,128)(2,1)} %get-tuple-element.29) | data formatting | bytes 1048576
  168.3 0.0 copy-done.1
  168.3 0.8 copy.18
  169.1 0.0 copy-done
  169.1 0.8 copy.19
Async XLA Ops:
  164.4 3.9 %copy-start.1 = (bf16[128,2048]{1,0:T(8,128)(2,1)S(1)}, bf16[128,2048]{1,0:T(8,128)(2,1)}, u32[]{:S(2)}) copy-start(bf16[128,2048]{1,0:T(8,128)(2,1)} %get-tuple-element.30) | copy-start | bytes 1572868
  164.5 4.7 %copy-start = (bf16[128,2048]{1,0:T(8,128)(2,1)S(1)}, bf16[128,2048]{1,0:T(8,128)(2,1)}, u32[]{:S(2)}) copy-start(bf16[128,2048]{1,0:T(8,128)(2,1)} %get-tuple-element.31) | copy-start | bytes 1572868

commit v2 on v1

v2 whole, which is shorter than its diff:
```python
import functools

import jax
import jax.numpy as jnp
import numpy as np
from jax import lax
from jax.sharding import PartitionSpec as P
import jax.experimental.pallas as pl
import jax.experimental.pallas.tpu as pltpu

HD = 128
HEADS = 16
TILE = 256
SP = 8
W = 6
HALF = 128
NONE = SP * W
MESH = pl.DeviceIdType.MESH
BF = jnp.bfloat16
F32 = jnp.float32
SCALE = HD**-0.5
SCALE2 = float(SCALE * np.log2(np.e))
NN = (((1,), (0,)), ((), ()))
TN = (((0,), (0,)), ((), ()))


def dot(a, b, dims):
    return lax.dot_general(a, b, dims, preferred_element_type=F32)


class Place:
    def __init__(self):
        self.tm = lax.axis_index("tm")
        self.index = lax.axis_index("head")
        self.low, self.y = self.tm // 4, lax.rem(self.tm, 4)
        x = self.index // 8
        z = 2 * lax.rem(self.index // 2, 4) + self.low
        self.half, self.mine = self.index // HEADS, lax.rem(self.index, HEADS)
        self.core = lax.rem(self.index, 2)
        self.head = 8 * (x // 2) + z
        self.group = 4 * lax.rem(x + z, 2) + self.y
        self.slice = 2 * self.group + self.core
        self.last = 2 * lax.axis_size("tm") - 1
        self.stays = (self.group == self.tm) & (self.core == self.half)

    def worker(self, group, head, core):
        z = lax.rem(head, 8)
        x = 2 * (head // 8) + lax.rem(group // 4 + z, 2)
        return 4 * lax.rem(z, 2) + lax.rem(group, 4), 8 * x + 2 * (z // 2) + core

    def worker_of_mine(self, head):
        return self.worker(self.tm, head, self.half)

    def holder(self, i):
        return self.group, HEADS * self.core + i

    def is_me(self, device):
        return (device[0] == self.tm) & (device[1] == self.index)

    def nth_head(self, n):
        step = n // 2
        far = (step + 1) // 2
        turn = jnp.where(lax.rem(step, 2) == 1, far, 8 - far)
        return 8 * lax.rem(self.head // 8 + n, 2) + lax.rem(self.head + turn, 8)

    def before(self):
        return self.worker(self.group - 1 + self.core, self.head, 1 - self.core)

    def after(self):
        return self.worker(self.group + self.core, self.head, 1 - self.core)


def greet(me):
    barrier = pltpu.get_barrier_semaphore()

    def signal(i):
        for other in (me.worker_of_mine(i), me.holder(i)):

            @pl.when(jnp.logical_not(me.is_me(other)))
            def _():
                pl.semaphore_signal(barrier, 1, device_id=other, device_id_type=MESH)

    loop(HEADS, signal)
    has_before, has_after = me.slice > 0, me.slice < me.last

    @pl.when(has_before)
    def _():
        pl.semaphore_signal(barrier, 1, device_id=me.before(), device_id_type=MESH)

    @pl.when(has_after)
    def _():
        pl.semaphore_signal(barrier, 1, device_id=me.after(), device_id_type=MESH)

    own = jnp.where(me.stays, 2, 0)
    pl.semaphore_wait(barrier, 2 * HEADS - own + has_before.astype(jnp.int32) + has_after.astype(jnp.int32))


def landed(ref, sem):
    pltpu.make_async_copy(ref, ref, sem).wait()


def send(src, dst, send_sem, recv_sem, target):
    pltpu.make_async_remote_copy(
        src_ref=src, dst_ref=dst, send_sem=send_sem, recv_sem=recv_sem, device_id=target, device_id_type=MESH
    ).start()


def half_rows(ref, i, first=0):
    return ref.at[first + i // 2, pl.ds(pl.multiple_of(lax.rem(i, 2) * HALF, HALF), HALF)]


def head_columns(ref, h):
    return ref.at[:, pl.ds(pl.multiple_of(h * HD, HD), HD)]


def loop(n, step):
    def body(i, carry):
        step(i)
        return carry

    lax.fori_loop(0, n, body, 0)


def tables(me, windows, tile_place, inverse, key_at, usable, query_of, pair_of):
    slice_id, last = me.slice, me.last

    def invert(n):
        near = jnp.clip(slice_id - 1 + n // SP, 0, last)
        tile = lax.rem(n, SP)
        found = jnp.int32(0)
        for i in range(SP):
            found = jnp.where(tile_place[near, i] == tile, i, found)
        inverse[n] = found

    loop(3 * SP, invert)

    def query(n):
        i = n // W
        w = lax.rem(n, W)
        tile = SP * slice_id + jnp.clip(tile_place[slice_id, i], 0, SP - 1)
        listed = windows[tile, w]
        good = listed >= 0
        named = jnp.where(good, listed, windows[tile, 2])
        near = jnp.clip(named - SP * (slice_id - 1), 0, 3 * SP - 1)
        key_at[n] = inverse[near] + SP * jnp.where(good, w // 2, 1)
        usable[n] = good.astype(jnp.int32)

    loop(SP * W, query)

    def key(n):
        m = n // 3
        j = m // SP
        near = jnp.clip(slice_id - 1 + j, 0, last)
        tile = jnp.clip(tile_place[near, lax.rem(m, SP)], 0, SP - 1)
        row = tile // 2 + lax.rem(n, 3) - 1
        inside = (row >= 0) & (row < SP // 2)
        asker = jnp.where(inside, 2 * row + lax.rem(tile, 2), 0)
        i = inverse[SP + asker]
        name = SP * near + tile
        first = windows[SP * slice_id + asker, 2 * j] == name
        second = windows[SP * slice_id + asker, 2 * j + 1] == name
        query_of[n] = i
        pair_of[n] = jnp.where(
            inside & (first | second), i * W + 2 * j + jnp.where(second, 1, 0), NONE
        )

    loop(9 * SP, key)


def query_tile(i, key_at, usable, q, g, kx, vx, o, dq, probs, dscores, q_scaled, g_scaled):
    q_rows = q[i]
    g_rows = g[i]
    q_turned = q_rows.T
    g_turned = g_rows.T
    at = [key_at[i * W + w] for w in range(W)]
    scores = [dot(kx[at[w]], q_turned, NN) for w in range(W)]
    peak = scores[0]
    for w in range(1, W):
        peak = jnp.maximum(peak, scores[w])
    peak = jnp.max(peak, axis=0, keepdims=True) * SCALE2
    total = jnp.zeros((1, TILE), F32)
    out = jnp.zeros((HD, TILE), F32)
    raised = []
    for w in range(W):
        level = peak + jnp.where(usable[i * W + w] > 0, 0.0, 1e30)
        e = jnp.exp2(scores[w] * SCALE2 - level)
        total = total + jnp.sum(e, axis=0, keepdims=True)
        low = e.astype(BF)
        probs[i * W + w] = low
        raised.append(e)
        out = out + dot(vx[at[w]], low, TN)
    share = 1.0 / total
    out_low = (out * share).astype(BF)
    o[i] = out_low.T
    row_term = jnp.sum(g_turned.astype(F32) * out_low.astype(F32), axis=0, keepdims=True)
    grad = jnp.zeros((HD, TILE), F32)
    for w in range(W):
        dprobs = dot(vx[at[w]], g_turned, NN)
        low = (raised[w] * (dprobs - row_term)).astype(BF)
        dscores[i * W + w] = low
        grad = grad + dot(kx[at[w]], low, TN)
    dq[i] = (grad * (share * SCALE)).astype(BF).T
    share_rows = jnp.transpose(jnp.broadcast_to(share, (HD, TILE)))
    q_scaled[i] = (q_rows.astype(F32) * (share_rows * SCALE)).astype(BF)
    g_scaled[i] = (g_rows.astype(F32) * share_rows).astype(BF)


def key_tile(m, query_of, pair_of, q_scaled, g_scaled, probs, dscores):
    grad_k = jnp.zeros((TILE, HD), F32)
    grad_v = jnp.zeros((TILE, HD), F32)
    for n in range(3):
        i = query_of[3 * m + n]
        pair = pair_of[3 * m + n]
        grad_v = grad_v + dot(probs[pair], g_scaled[i], NN)
        grad_k = grad_k + dot(dscores[pair], q_scaled[i], NN)
    return grad_k, grad_v


def attention_kernel(
    windows, tile_place, q_in, k_in, v_in, g_in, o_out, dq_out, dk_out, dv_out,
    q, kx, vx, g, o, dq, probs, dscores, q_scaled, g_scaled, dk_far, dv_far, dk_near, dv_near, dk_low, dv_low,
    inverse, key_at, usable, query_of, pair_of, sent, got, halo_sent, halo_got,
):
    me = Place()
    has_before, has_after = me.slice > 0, me.slice < me.last
    greet(me)

    arrivals = ((k_in, kx, SP), (v_in, vx, SP), (q_in, q, 0), (g_in, g, 0))
    for a, (src, dst, first) in enumerate(arrivals):

        def push(n):
            h = me.nth_head(n)
            target = me.worker_of_mine(h)
            to = half_rows(dst, me.mine, first)

            @pl.when(jnp.logical_not(me.is_me(target)))
            def _():
                send(head_columns(src, h), to, sent.at[a, h], got.at[a, me.mine], target)

            @pl.when(me.is_me(target))
            def _():
                pltpu.make_async_copy(head_columns(src, h), to, got.at[a, me.mine]).start()

        loop(HEADS, push)

    tables(me, windows, tile_place, inverse, key_at, usable, query_of, pair_of)
    probs[NONE] = jnp.zeros((TILE, TILE), BF)
    dscores[NONE] = jnp.zeros((TILE, TILE), BF)

    def exchange(a, to_before, to_after, from_before, from_after):
        @pl.when(has_before)
        def _():
            send(to_before, from_after, halo_sent.at[a, 0], halo_got.at[a, 1], me.before())

        @pl.when(has_after)
        def _():
            send(to_after, from_before, halo_sent.at[a, 1], halo_got.at[a, 0], me.after())

    def exchanged(a, to_before, to_after, from_before, from_after):
        @pl.when(has_before)
        def _():
            landed(from_before, halo_got.at[a, 0])
            landed(to_before, halo_sent.at[a, 0])

        @pl.when(has_after)
        def _():
            landed(from_after, halo_got.at[a, 1])
            landed(to_after, halo_sent.at[a, 1])

    def key_halo(x):
        own = x.at[pl.ds(SP, SP)]
        return own, own, x.at[pl.ds(0, SP)], x.at[pl.ds(2 * SP, SP)]

    def grad_halo(far, near):
        first, second = pl.ds(0, SP), pl.ds(SP, SP)
        return far.at[first], far.at[second], near.at[first], near.at[second]

    for a, x in enumerate((kx, vx)):
        loop(HEADS, lambda i: landed(half_rows(x, i, SP), got.at[a, i]))
        exchange(a, *key_halo(x))
    for a, x in enumerate((kx, vx)):
        exchanged(a, *key_halo(x))

    def push_back(a, src, dst, i):
        target = me.holder(i)
        to = head_columns(dst, me.head)

        @pl.when(jnp.logical_not(me.is_me(target)))
        def _():
            send(half_rows(src, i), to, sent.at[a, i], got.at[a, me.head], target)

        @pl.when(me.is_me(target))
        def _():
            pltpu.make_async_copy(half_rows(src, i), to, got.at[a, me.head]).start()

    def query_step(i):
        for part in (2 * i, 2 * i + 1):
            landed(half_rows(q, part), got.at[2, part])
            landed(half_rows(g, part), got.at[3, part])
        query_tile(i, key_at, usable, q, g, kx, vx, o, dq, probs, dscores, q_scaled, g_scaled)
        for part in (2 * i, 2 * i + 1):
            push_back(4, o, o_out, part)
            push_back(5, dq, dq_out, part)

    loop(SP, query_step)

    def far_step(n):
        m = jnp.where(n < SP, n, n + SP)
        grad_k, grad_v = key_tile(m, query_of, pair_of, q_scaled, g_scaled, probs, dscores)
        dk_far[n] = grad_k.astype(BF)
        dv_far[n] = grad_v.astype(BF)

    loop(2 * SP, far_step)
    halos = (grad_halo(dk_far, dk_near), grad_halo(dv_far, dv_near))
    for a, halo in enumerate(halos):
        exchange(2 + a, *halo)

    @pl.when(jnp.logical_not(has_before))
    def _():
        for near in (dk_near, dv_near):
            near[pl.ds(0, SP)] = jnp.zeros((SP, TILE, HD), BF)

    @pl.when(jnp.logical_not(has_after))
    def _():
        for near in (dk_near, dv_near):
            near[pl.ds(SP, SP)] = jnp.zeros((SP, TILE, HD), BF)

    for a, halo in enumerate(halos):
        exchanged(2 + a, *halo)

    def own_step(m):
        grad_k, grad_v = key_tile(SP + m, query_of, pair_of, q_scaled, g_scaled, probs, dscores)
        dk_low[m] = (grad_k + dk_near[m].astype(F32) + dk_near[SP + m].astype(F32)).astype(BF)
        dv_low[m] = (grad_v + dv_near[m].astype(F32) + dv_near[SP + m].astype(F32)).astype(BF)
        for part in (2 * m, 2 * m + 1):
            push_back(6, dk_low, dk_out, part)
            push_back(7, dv_low, dv_out, part)

    loop(SP, own_step)

    for a, (_, dst, first) in enumerate(arrivals):

        def drain(n):
            @pl.when(jnp.logical_not(me.is_me(me.worker_of_mine(n))))
            def _():
                landed(half_rows(dst, me.mine, first), sent.at[a, n])

        loop(HEADS, drain)

    for a, (src, dst) in enumerate(((o, o_out), (dq, dq_out), (dk_low, dk_out), (dv_low, dv_out))):

        def finish(i):
            landed(head_columns(dst, i), got.at[4 + a, i])

            @pl.when(jnp.logical_not(me.is_me(me.holder(i))))
            def _():
                landed(half_rows(src, i), sent.at[4 + a, i])

        loop(HEADS, finish)


def body(queries, key_rows, value_rows, grad_out, windows, tile_place):
    anywhere = pl.BlockSpec(memory_space=pl.ANY)
    smem = pl.BlockSpec(memory_space=pltpu.SMEM)
    tiles = lambda n: pltpu.VMEM((n, TILE, HD), BF)
    pairs = pltpu.VMEM((NONE + 1, TILE, TILE), BF)
    numbers = lambda n: pltpu.SMEM((n,), jnp.int32)
    dma = pltpu.SemaphoreType.DMA
    rows = jax.ShapeDtypeStruct(queries.shape, BF)
    return pl.pallas_call(
        attention_kernel,
        out_shape=[rows] * 4,
        in_specs=[smem] * 2 + [anywhere] * 4,
        out_specs=[anywhere] * 4,
        scratch_shapes=[tiles(SP), tiles(3 * SP), tiles(3 * SP), tiles(SP), tiles(SP), tiles(SP), pairs, pairs]
        + [tiles(SP)] * 2
        + [tiles(2 * SP)] * 4
        + [tiles(SP)] * 2
        + [numbers(3 * SP), numbers(SP * W), numbers(SP * W), numbers(9 * SP), numbers(9 * SP)]
        + [dma((8, HEADS)), dma((8, HEADS)), dma((4, 2)), dma((4, 2))],
        compiler_params=pltpu.CompilerParams(
            collective_id=0, has_side_effects=True, vmem_limit_bytes=56 * 1024 * 1024
        ),
        name="attention",
    )(windows, tile_place, queries, key_rows, value_rows, grad_out)


def solution(mesh):
    spread = P(("tm", "head"), None)
    return jax.shard_map(
        body,
        mesh=mesh,
        in_specs=(spread,) * 4 + (P(), P()),
        out_specs=(spread,) * 4,
        check_vma=False,
    )
```

time: 173 us -> 130 us (0.75); the launches traced: 170 us -> 130 us
  Pallas kernels: 161 us -> 122 us
    pallas_call x3 -> x1, Pallas kernels: 161 us -> 122 us  [body(): pl.pallas_call(attention_kernel, out_shape=[rows] * 4, in_specs=[smem] *...]
    unnamed x10 -> x14, local copies, waits for them, and re-layouts: 8.22 us -> 7.3 us
where the time goes in v2:
time: 130 us
  Pallas kernels  122 us (94%)
  local copies, waits for them, and re-layouts  7.3 us (6%)
    pallas_call x1, Pallas kernels, body(): pl.pallas_call(attention_kernel, out_shape=[rows] * 4, in_specs=[smem] *...  122 us
    unnamed x14, local copies, waits for them, and re-layouts  7.3 us

profile of v2, /device:TPU:35, one launch (start us, length us, event | category | flops | bytes accessed | tf_op | source)
XLA Modules:
  0.0 129.8 jit_solution(2578082927693498005)
XLA Ops:
  0.6 0.0 copy-start.3
  0.6 1.4 %copy.11.tile_place = s32[16,8]{1,0:T(8,128)} copy(s32[16,8]{0,1:T(8,128)} %param.11) | data formatting | bytes 1024 | tf_op args[5]
  2.0 0.0 copy-done.3
  2.0 0.7 copy.10.windows
  2.7 121.9 %attention.1 = (bf16[128,2048]{1,0:T(8,128)(2,1)}, bf16[128,2048]{1,0:T(8,128)(2,1)}, bf16[128,2048]{1,0:T(8,128)(2,1)}, bf16[128,2048]{1,0:T(8,128)(2,1)}) custom-call(s32[128,6]{1,0:T(8,128)} %copy.10.windows, s32[16,8]{1,0:T(8,128)} %copy.11.tile_place, bf16[128,2048]{1,0:T(8,128)(2,1)} %q_in.1, bf16[128,2048]{1,0:T(8,128)(2,1)} %k_in.1, ...), custom_call_target="tpu_custom_call" | custom-call | tf_op jit(solution)/shard_map/attention/pallas_call | solution.py:370
  124.6 0.0 copy-start.2
  124.6 1.9 %copy.16 = bf16[128,2048]{1,0:T(8,128)(2,1)} copy(bf16[128,2048]{1,0:T(8,128)(2,1)} %get-tuple-element.8) | data formatting | bytes 1048576
  126.6 0.0 copy-done.2
  126.6 0.0 copy-start.1
  126.6 0.8 copy.17
  127.4 0.4 copy-done.1
  127.8 0.0 copy-start
  127.8 0.8 copy.18
  128.6 0.4 copy-done
  129.0 0.8 copy.19
Async XLA Ops:
  0.6 1.4 %copy-start.3 = (s32[128,6]{0,1:T(8,128)S(1)}, s32[128,6]{0,1:T(8,128)}, u32[]{:S(2)}) copy-start(s32[128,6]{0,1:T(8,128)} %param.10) | copy-start | bytes 9220
  124.6 2.0 %copy-start.2 = (bf16[128,2048]{1,0:T(8,128)(2,1)S(1)}, bf16[128,2048]{1,0:T(8,128)(2,1)}, u32[]{:S(2)}) copy-start(bf16[128,2048]{1,0:T(8,128)(2,1)} %get-tuple-element.9) | copy-start | bytes 1572868
  126.6 1.2 copy-start.1
  127.8 1.2 copy-start

commit v3 on v2

--- a/solution.py
+++ b/solution.py
@@ -33,8 +33,8 @@
         self.tm = lax.axis_index("tm")
         self.index = lax.axis_index("head")
         self.low, self.y = self.tm // 4, lax.rem(self.tm, 4)
-        x = self.index // 8
-        z = 2 * lax.rem(self.index // 2, 4) + self.low
+        self.x = x = self.index // 8
+        self.z = z = 2 * lax.rem(self.index // 2, 4) + self.low
         self.half, self.mine = self.index // HEADS, lax.rem(self.index, HEADS)
         self.core = lax.rem(self.index, 2)
         self.head = 8 * (x // 2) + z
@@ -63,6 +63,14 @@
         turn = jnp.where(lax.rem(step, 2) == 1, far, 8 - far)
         return 8 * lax.rem(self.head // 8 + n, 2) + lax.rem(self.head + turn, 8)
 
+    def nth_tile(self, n):
+        step = n // 2
+        even = lax.rem(self.z + self.group // 4, 2) == 0
+        near = jnp.where(even, jnp.where(step == 1, 2, 0), jnp.where(step == 1, 7, 1))
+        far = jnp.where(even, jnp.where(step == 2, 6, 4), jnp.where(step == 2, 3, 5))
+        z = lax.rem(self.z + jnp.where(step < 2, near, far), 8)
+        return 4 * lax.rem(self.x + n, 2) + z // 2
+
     def before(self):
         return self.worker(self.group - 1 + self.core, self.head, 1 - self.core)
 
@@ -129,7 +137,7 @@
         tile = lax.rem(n, SP)
         found = jnp.int32(0)
         for i in range(SP):
-            found = jnp.where(tile_place[near, i] == tile, i, found)
+            found = jnp.where(tile_place[i, near] == tile, i, found)
         inverse[n] = found
 
     loop(3 * SP, invert)
@@ -137,10 +145,10 @@
     def query(n):
         i = n // W
         w = lax.rem(n, W)
-        tile = SP * slice_id + jnp.clip(tile_place[slice_id, i], 0, SP - 1)
-        listed = windows[tile, w]
+        tile = SP * slice_id + jnp.clip(tile_place[i, slice_id], 0, SP - 1)
+        listed = windows[w, tile]
         good = listed >= 0
-        named = jnp.where(good, listed, windows[tile, 2])
+        named = jnp.where(good, listed, windows[2, tile])
         near = jnp.clip(named - SP * (slice_id - 1), 0, 3 * SP - 1)
         key_at[n] = inverse[near] + SP * jnp.where(good, w // 2, 1)
         usable[n] = good.astype(jnp.int32)
@@ -151,14 +159,14 @@
         m = n // 3
         j = m // SP
         near = jnp.clip(slice_id - 1 + j, 0, last)
-        tile = jnp.clip(tile_place[near, lax.rem(m, SP)], 0, SP - 1)
+        tile = jnp.clip(tile_place[lax.rem(m, SP), near], 0, SP - 1)
         row = tile // 2 + lax.rem(n, 3) - 1
         inside = (row >= 0) & (row < SP // 2)
         asker = jnp.where(inside, 2 * row + lax.rem(tile, 2), 0)
         i = inverse[SP + asker]
         name = SP * near + tile
-        first = windows[SP * slice_id + asker, 2 * j] == name
-        second = windows[SP * slice_id + asker, 2 * j + 1] == name
+        first = windows[2 * j, SP * slice_id + asker] == name
+        second = windows[2 * j + 1, SP * slice_id + asker] == name
         query_of[n] = i
         pair_of[n] = jnp.where(
             inside & (first | second), i * W + 2 * j + jnp.where(second, 1, 0), NONE
@@ -167,11 +175,9 @@
     loop(9 * SP, key)
 
 
-def query_tile(i, key_at, usable, q, g, kx, vx, o, dq, probs, dscores, q_scaled, g_scaled):
+def forward_tile(i, key_at, usable, q, kx, vx, o, o_turned, share, probs, q_scaled):
     q_rows = q[i]
-    g_rows = g[i]
     q_turned = q_rows.T
-    g_turned = g_rows.T
     at = [key_at[i * W + w] for w in range(W)]
     scores = [dot(kx[at[w]], q_turned, NN) for w in range(W)]
     peak = scores[0]
@@ -180,29 +186,37 @@
     peak = jnp.max(peak, axis=0, keepdims=True) * SCALE2
     total = jnp.zeros((1, TILE), F32)
     out = jnp.zeros((HD, TILE), F32)
-    raised = []
     for w in range(W):
         level = peak + jnp.where(usable[i * W + w] > 0, 0.0, 1e30)
         e = jnp.exp2(scores[w] * SCALE2 - level)
         total = total + jnp.sum(e, axis=0, keepdims=True)
         low = e.astype(BF)
         probs[i * W + w] = low
-        raised.append(e)
         out = out + dot(vx[at[w]], low, TN)
-    share = 1.0 / total
-    out_low = (out * share).astype(BF)
+    part = 1.0 / total
+    out_low = (out * part).astype(BF)
+    share[i] = part
+    o_turned[i] = out_low
     o[i] = out_low.T
-    row_term = jnp.sum(g_turned.astype(F32) * out_low.astype(F32), axis=0, keepdims=True)
+    part_rows = jnp.transpose(jnp.broadcast_to(part, (HD, TILE)))
+    q_scaled[i] = (q_rows.astype(F32) * (part_rows * SCALE)).astype(BF)
+
+
+def backward_tile(i, key_at, g, kx, vx, dq, o_turned, share, probs, dscores, g_scaled):
+    g_rows = g[i]
+    g_turned = g_rows.T
+    at = [key_at[i * W + w] for w in range(W)]
+    part = share[i]
+    row_term = jnp.sum(g_turned.astype(F32) * o_turned[i].astype(F32), axis=0, keepdims=True)
     grad = jnp.zeros((HD, TILE), F32)
     for w in range(W):
         dprobs = dot(vx[at[w]], g_turned, NN)
-        low = (raised[w] * (dprobs - row_term)).astype(BF)
+        low = (probs[i * W + w].astype(F32) * (dprobs - row_term)).astype(BF)
         dscores[i * W + w] = low
         grad = grad + dot(kx[at[w]], low, TN)
-    dq[i] = (grad * (share * SCALE)).astype(BF).T
-    share_rows = jnp.transpose(jnp.broadcast_to(share, (HD, TILE)))
-    q_scaled[i] = (q_rows.astype(F32) * (share_rows * SCALE)).astype(BF)
-    g_scaled[i] = (g_rows.astype(F32) * share_rows).astype(BF)
+    dq[i] = (grad * (part * SCALE)).astype(BF).T
+    part_rows = jnp.transpose(jnp.broadcast_to(part, (HD, TILE)))
+    g_scaled[i] = (g_rows.astype(F32) * part_rows).astype(BF)
 
 
 def key_tile(m, query_of, pair_of, q_scaled, g_scaled, probs, dscores):
@@ -218,15 +232,16 @@
 
 def attention_kernel(
     windows, tile_place, q_in, k_in, v_in, g_in, o_out, dq_out, dk_out, dv_out,
-    q, kx, vx, g, o, dq, probs, dscores, q_scaled, g_scaled, dk_far, dv_far, dk_near, dv_near, dk_low, dv_low,
-    inverse, key_at, usable, query_of, pair_of, sent, got, halo_sent, halo_got,
+    q, kx, vx, g, o, dq, o_turned, share, probs, dscores, q_scaled, g_scaled, dk_far, dv_far, dk_near, dv_near,
+    dk_low, dv_low, inverse, key_at, usable, query_of, pair_of, sent, got, halo_sent, halo_got, grad_sent, grad_got,
 ):
     me = Place()
     has_before, has_after = me.slice > 0, me.slice < me.last
     greet(me)
 
     arrivals = ((k_in, kx, SP), (v_in, vx, SP), (q_in, q, 0), (g_in, g, 0))
-    for a, (src, dst, first) in enumerate(arrivals):
+    def push_all(a):
+        src, dst, first = arrivals[a]
 
         def push(n):
             h = me.nth_head(n)
@@ -243,6 +258,8 @@
 
         loop(HEADS, push)
 
+    for a in (0, 1, 2, 3):
+        push_all(a)
     tables(me, windows, tile_place, inverse, key_at, usable, query_of, pair_of)
     probs[NONE] = jnp.zeros((TILE, TILE), BF)
     dscores[NONE] = jnp.zeros((TILE, TILE), BF)
@@ -271,16 +288,15 @@
         own = x.at[pl.ds(SP, SP)]
         return own, own, x.at[pl.ds(0, SP)], x.at[pl.ds(2 * SP, SP)]
 
-    def grad_halo(far, near):
-        first, second = pl.ds(0, SP), pl.ds(SP, SP)
-        return far.at[first], far.at[second], near.at[first], near.at[second]
+    def arrived(a):
+        _, dst, first = arrivals[a]
+        loop(HEADS, lambda i: landed(half_rows(dst, i, first), got.at[a, i]))
 
     for a, x in enumerate((kx, vx)):
-        loop(HEADS, lambda i: landed(half_rows(x, i, SP), got.at[a, i]))
+        arrived(a)
         exchange(a, *key_halo(x))
     for a, x in enumerate((kx, vx)):
         exchanged(a, *key_halo(x))
-
     def push_back(a, src, dst, i):
         target = me.holder(i)
         to = head_columns(dst, me.head)
@@ -293,27 +309,44 @@
         def _():
             pltpu.make_async_copy(half_rows(src, i), to, got.at[a, me.head]).start()
 
-    def query_step(i):
+    def forward_step(n):
+        i = me.nth_tile(n)
         for part in (2 * i, 2 * i + 1):
             landed(half_rows(q, part), got.at[2, part])
-            landed(half_rows(g, part), got.at[3, part])
-        query_tile(i, key_at, usable, q, g, kx, vx, o, dq, probs, dscores, q_scaled, g_scaled)
+        forward_tile(i, key_at, usable, q, kx, vx, o, o_turned, share, probs, q_scaled)
         for part in (2 * i, 2 * i + 1):
             push_back(4, o, o_out, part)
+
+    def backward_step(n):
+        i = me.nth_tile(n)
+        for part in (2 * i, 2 * i + 1):
+            landed(half_rows(g, part), got.at[3, part])
+        backward_tile(i, key_at, g, kx, vx, dq, o_turned, share, probs, dscores, g_scaled)
+        for part in (2 * i, 2 * i + 1):
             push_back(5, dq, dq_out, part)
 
-    loop(SP, query_step)
-
-    def far_step(n):
+    loop(SP, forward_step)
+    loop(SP, backward_step)
+
+    def far_step(k):
+        n = lax.rem(k + SP * me.core, 2 * SP)
         m = jnp.where(n < SP, n, n + SP)
         grad_k, grad_v = key_tile(m, query_of, pair_of, q_scaled, g_scaled, probs, dscores)
         dk_far[n] = grad_k.astype(BF)
         dv_far[n] = grad_v.astype(BF)
-
+        there = lax.rem(n + SP, 2 * SP)
+        for a, (far, near) in enumerate(grads):
+
+            @pl.when((n < SP) & has_before)
+            def _():
+                send(far.at[n], near.at[there], grad_sent.at[a, n], grad_got.at[a, there], me.before())
+
+            @pl.when((n >= SP) & has_after)
+            def _():
+                send(far.at[n], near.at[there], grad_sent.at[a, n], grad_got.at[a, there], me.after())
+
+    grads = ((dk_far, dk_near), (dv_far, dv_near))
     loop(2 * SP, far_step)
-    halos = (grad_halo(dk_far, dk_near), grad_halo(dv_far, dv_near))
-    for a, halo in enumerate(halos):
-        exchange(2 + a, *halo)
 
     @pl.when(jnp.logical_not(has_before))
     def _():
@@ -325,11 +358,19 @@
         for near in (dk_near, dv_near):
             near[pl.ds(SP, SP)] = jnp.zeros((SP, TILE, HD), BF)
 
-    for a, halo in enumerate(halos):
-        exchanged(2 + a, *halo)
-
-    def own_step(m):
+    def own_step(n):
+        m = me.nth_tile(n)
         grad_k, grad_v = key_tile(SP + m, query_of, pair_of, q_scaled, g_scaled, probs, dscores)
+        for a, (_, near) in enumerate(grads):
+
+            @pl.when(has_before)
+            def _():
+                landed(near.at[m], grad_got.at[a, m])
+
+            @pl.when(has_after)
+            def _():
+                landed(near.at[SP + m], grad_got.at[a, SP + m])
+
         dk_low[m] = (grad_k + dk_near[m].astype(F32) + dk_near[SP + m].astype(F32)).astype(BF)
         dv_low[m] = (grad_v + dv_near[m].astype(F32) + dv_near[SP + m].astype(F32)).astype(BF)
         for part in (2 * m, 2 * m + 1):
@@ -338,6 +379,15 @@
 
     loop(SP, own_step)
 
+    def drain_far(n):
+        for a, (far, _) in enumerate(grads):
+
+            @pl.when(jnp.where(n < SP, has_before, has_after))
+            def _():
+                landed(far.at[n], grad_sent.at[a, n])
+
+    loop(2 * SP, drain_far)
+
     for a, (_, dst, first) in enumerate(arrivals):
 
         def drain(n):
@@ -357,6 +407,19 @@
                 landed(half_rows(src, i), sent.at[4 + a, i])
 
         loop(HEADS, finish)
+
+
+def write_kernel(*refs):
+    sources, targets, held, sems = refs[:4], refs[4:8], refs[8:12], refs[12]
+    reads = [pltpu.make_async_copy(src, mid, sems.at[0, n]) for n, (src, mid) in enumerate(zip(sources, held))]
+    writes = [pltpu.make_async_copy(mid, dst, sems.at[1, n]) for n, (mid, dst) in enumerate(zip(held, targets))]
+    for read in reads:
+        read.start()
+    for read, write in zip(reads, writes):
+        read.wait()
+        write.start()
+    for write in writes:
+        write.wait()
 
 
 def body(queries, key_rows, value_rows, grad_out, windows, tile_place):
@@ -367,22 +430,31 @@
     numbers = lambda n: pltpu.SMEM((n,), jnp.int32)
     dma = pltpu.SemaphoreType.DMA
     rows = jax.ShapeDtypeStruct(queries.shape, BF)
-    return pl.pallas_call(
+    results = pl.pallas_call(
         attention_kernel,
         out_shape=[rows] * 4,
         in_specs=[smem] * 2 + [anywhere] * 4,
         out_specs=[anywhere] * 4,
-        scratch_shapes=[tiles(SP), tiles(3 * SP), tiles(3 * SP), tiles(SP), tiles(SP), tiles(SP), pairs, pairs]
+        scratch_shapes=[tiles(SP), tiles(3 * SP), tiles(3 * SP), tiles(SP), tiles(SP), tiles(SP)]
+        + [pltpu.VMEM((SP, HD, TILE), BF), pltpu.VMEM((SP, 1, TILE), F32), pairs, pairs]
         + [tiles(SP)] * 2
         + [tiles(2 * SP)] * 4
         + [tiles(SP)] * 2
         + [numbers(3 * SP), numbers(SP * W), numbers(SP * W), numbers(9 * SP), numbers(9 * SP)]
-        + [dma((8, HEADS)), dma((8, HEADS)), dma((4, 2)), dma((4, 2))],
+        + [dma((8, HEADS)), dma((8, HEADS)), dma((2, 2)), dma((2, 2)), dma((2, 2 * SP)), dma((2, 2 * SP))],
         compiler_params=pltpu.CompilerParams(
             collective_id=0, has_side_effects=True, vmem_limit_bytes=56 * 1024 * 1024
         ),
         name="attention",
-    )(windows, tile_place, queries, key_rows, value_rows, grad_out)
+    )(windows.T, tile_place.T, queries, key_rows, value_rows, grad_out)
+    return pl.pallas_call(
+        write_kernel,
+        out_shape=[rows] * 4,
+        in_specs=[anywhere] * 4,
+        out_specs=[anywhere] * 4,
+        scratch_shapes=[pltpu.VMEM(queries.shape, BF)] * 4 + [dma((2, 4))],
+        name="write",
+    )(*results)
 
 
 def solution(mesh):

time: 130 us -> 114 us (0.88); the launches traced: 130 us -> 112 us
  Pallas kernels: 122 us -> 112 us
  local copies, waits for them, and re-layouts: 7.3 us -> 0 us
    pallas_call x1, Pallas kernels: 122 us -> 109 us  [body(): pl.pallas_call(attention_kernel, out_shape=[rows] * 4, in_specs=[smem] *...]
    unnamed x14 -> x0, local copies, waits for them, and re-layouts: 7.3 us -> none
    pallas_call x0 -> x1, Pallas kernels: none -> 2.42 us  [body(): pl.pallas_call(write_kernel, out_shape=[rows] * 4, in_specs=[anywhere] *...]
where the time goes in v3:
time: 114 us; the launch traced here: 112 us
  Pallas kernels  112 us (98%)
    pallas_call x1, Pallas kernels, body(): pl.pallas_call(attention_kernel, out_shape=[rows] * 4, in_specs=[smem] *...  109 us
    pallas_call x1, Pallas kernels, body(): pl.pallas_call(write_kernel, out_shape=[rows] * 4, in_specs=[anywhere] *...  2.42 us

profile of v3, /device:TPU:35, one launch (start us, length us, event | category | flops | bytes accessed | tf_op | source)
XLA Modules:
  0.0 112.4 jit_solution(11452231436142436520)
XLA Ops:
  0.6 109.4 %attention.1 = (bf16[128,2048]{1,0:T(8,128)(2,1)}, bf16[128,2048]{1,0:T(8,128)(2,1)}, bf16[128,2048]{1,0:T(8,128)(2,1)}, bf16[128,2048]{1,0:T(8,128)(2,1)}) custom-call(s32[6,128]{1,0:T(8,128)} %bitcast.2, s32[8,16]{1,0:T(8,128)} %bitcast.3, bf16[128,2048]{1,0:T(8,128)(2,1)} %q_in.1, bf16[128,2048]{1,0:T(8,128)(2,1)} %k_in.1, bf16[128,2048]{1,0:T(8,128)(2,1)} %v_in.1, ...), custom_call_target="tpu_custom_call" | custom-call | tf_op jit(solution)/shard_map/attention/pallas_call | solution.py:433
  110.0 2.4 %write.1 = (bf16[128,2048]{1,0:T(8,128)(2,1)}, bf16[128,2048]{1,0:T(8,128)(2,1)}, bf16[128,2048]{1,0:T(8,128)(2,1)}, bf16[128,2048]{1,0:T(8,128)(2,1)}) custom-call(bf16[128,2048]{1,0:T(8,128)(2,1)} %get-tuple-element.8.refs_0_, bf16[128,2048]{1,0:T(8,128)(2,1)} %get-tuple-element.9.refs_1_, bf16[128,2048]{1,0:T(8,128)(2,1)} %get-tuple-element.10.refs_2_, ...), custom_call_target="tpu_custom_call" | custom-call | tf_op jit(solution)/shard_map/write/pallas_call | solution.py:450

commit v4 on v3

--- a/solution.py
+++ b/solution.py
@@ -244,7 +244,7 @@
         src, dst, first = arrivals[a]
 
         def push(n):
-            h = me.nth_head(n)
+            h = me.nth_head(HEADS - 1 - n)
             target = me.worker_of_mine(h)
             to = half_rows(dst, me.mine, first)
 
@@ -264,39 +264,38 @@
     probs[NONE] = jnp.zeros((TILE, TILE), BF)
     dscores[NONE] = jnp.zeros((TILE, TILE), BF)
 
-    def exchange(a, to_before, to_after, from_before, from_after):
+    def pass_on(a, n):
+        src, x, first = arrivals[a]
+        i = me.nth_tile(SP - 1 - n)
+        for part in (2 * i, 2 * i + 1):
+            landed(half_rows(x, part, SP), got.at[a, part])
+
         @pl.when(has_before)
         def _():
-            send(to_before, from_after, halo_sent.at[a, 0], halo_got.at[a, 1], me.before())
+            send(x.at[SP + i], x.at[2 * SP + i], halo_sent.at[a, i], halo_got.at[a, SP + i], me.before())
 
         @pl.when(has_after)
         def _():
-            send(to_after, from_before, halo_sent.at[a, 1], halo_got.at[a, 0], me.after())
-
-    def exchanged(a, to_before, to_after, from_before, from_after):
+            send(x.at[SP + i], x.at[i], halo_sent.at[a, SP + i], halo_got.at[a, i], me.after())
+
+    def passed_on(a, i):
+        x = arrivals[a][1]
+
         @pl.when(has_before)
         def _():
-            landed(from_before, halo_got.at[a, 0])
-            landed(to_before, halo_sent.at[a, 0])
+            landed(x.at[i], halo_got.at[a, i])
+            landed(x.at[SP + i], halo_sent.at[a, i])
 
         @pl.when(has_after)
         def _():
-            landed(from_after, halo_got.at[a, 1])
-            landed(to_after, halo_sent.at[a, 1])
-
-    def key_halo(x):
-        own = x.at[pl.ds(SP, SP)]
-        return own, own, x.at[pl.ds(0, SP)], x.at[pl.ds(2 * SP, SP)]
-
-    def arrived(a):
-        _, dst, first = arrivals[a]
-        loop(HEADS, lambda i: landed(half_rows(dst, i, first), got.at[a, i]))
-
-    for a, x in enumerate((kx, vx)):
-        arrived(a)
-        exchange(a, *key_halo(x))
-    for a, x in enumerate((kx, vx)):
-        exchanged(a, *key_halo(x))
+            landed(x.at[2 * SP + i], halo_got.at[a, SP + i])
+            landed(x.at[SP + i], halo_sent.at[a, SP + i])
+
+    for a in (0, 1):
+        loop(SP, functools.partial(pass_on, a))
+    for a in (0, 1):
+        loop(SP, functools.partial(passed_on, a))
+
     def push_back(a, src, dst, i):
         target = me.holder(i)
         to = head_columns(dst, me.head)
@@ -310,7 +309,7 @@
             pltpu.make_async_copy(half_rows(src, i), to, got.at[a, me.head]).start()
 
     def forward_step(n):
-        i = me.nth_tile(n)
+        i = me.nth_tile(SP - 1 - n)
         for part in (2 * i, 2 * i + 1):
             landed(half_rows(q, part), got.at[2, part])
         forward_tile(i, key_at, usable, q, kx, vx, o, o_turned, share, probs, q_scaled)
@@ -318,7 +317,7 @@
             push_back(4, o, o_out, part)
 
     def backward_step(n):
-        i = me.nth_tile(n)
+        i = me.nth_tile(SP - 1 - n)
         for part in (2 * i, 2 * i + 1):
             landed(half_rows(g, part), got.at[3, part])
         backward_tile(i, key_at, g, kx, vx, dq, o_turned, share, probs, dscores, g_scaled)
@@ -359,7 +358,7 @@
             near[pl.ds(SP, SP)] = jnp.zeros((SP, TILE, HD), BF)
 
     def own_step(n):
-        m = me.nth_tile(n)
+        m = me.nth_tile(SP - 1 - n)
         grad_k, grad_v = key_tile(SP + m, query_of, pair_of, q_scaled, g_scaled, probs, dscores)
         for a, (_, near) in enumerate(grads):
 
@@ -441,7 +440,7 @@
         + [tiles(2 * SP)] * 4
         + [tiles(SP)] * 2
         + [numbers(3 * SP), numbers(SP * W), numbers(SP * W), numbers(9 * SP), numbers(9 * SP)]
-        + [dma((8, HEADS)), dma((8, HEADS)), dma((2, 2)), dma((2, 2)), dma((2, 2 * SP)), dma((2, 2 * SP))],
+        + [dma((8, HEADS)), dma((8, HEADS)), dma((2, 2 * SP)), dma((2, 2 * SP)), dma((2, 2 * SP)), dma((2, 2 * SP))],
         compiler_params=pltpu.CompilerParams(
             collective_id=0, has_side_effects=True, vmem_limit_bytes=56 * 1024 * 1024
         ),

time: 114 us -> 111 us (0.974)
  Pallas kernels: 112 us -> 109 us
    pallas_call x1, Pallas kernels: 109 us -> 107 us  [body(): pl.pallas_call(attention_kernel, out_shape=[rows] * 4, in_specs=[smem] *...]
where the time goes in v4:
time: 111 us; the launch traced here: 110 us
  Pallas kernels  109 us (98%)
    pallas_call x1, Pallas kernels, body(): pl.pallas_call(attention_kernel, out_shape=[rows] * 4, in_specs=[smem] *...  107 us
    pallas_call x1, Pallas kernels, body(): pl.pallas_call(write_kernel, out_shape=[rows] * 4, in_specs=[anywhere] *...  2.42 us

profile of v4, /device:TPU:35, one launch (start us, length us, event | category | flops | bytes accessed | tf_op | source)
XLA Modules:
  0.0 109.7 jit_solution(802086222415046676)
XLA Ops:
  0.6 106.6 %attention.1 = (bf16[128,2048]{1,0:T(8,128)(2,1)}, bf16[128,2048]{1,0:T(8,128)(2,1)}, bf16[128,2048]{1,0:T(8,128)(2,1)}, bf16[128,2048]{1,0:T(8,128)(2,1)}) custom-call(s32[6,128]{1,0:T(8,128)} %bitcast.2, s32[8,16]{1,0:T(8,128)} %bitcast.3, bf16[128,2048]{1,0:T(8,128)(2,1)} %q_in.1, bf16[128,2048]{1,0:T(8,128)(2,1)} %k_in.1, bf16[128,2048]{1,0:T(8,128)(2,1)} %v_in.1, ...), custom_call_target="tpu_custom_call" | custom-call | tf_op jit(solution)/shard_map/attention/pallas_call | solution.py:432
  107.2 2.4 %write.1 = (bf16[128,2048]{1,0:T(8,128)(2,1)}, bf16[128,2048]{1,0:T(8,128)(2,1)}, bf16[128,2048]{1,0:T(8,128)(2,1)}, bf16[128,2048]{1,0:T(8,128)(2,1)}) custom-call(bf16[128,2048]{1,0:T(8,128)(2,1)} %get-tuple-element.8.refs_0_, bf16[128,2048]{1,0:T(8,128)(2,1)} %get-tuple-element.9.refs_1_, bf16[128,2048]{1,0:T(8,128)(2,1)} %get-tuple-element.10.refs_2_, ...), custom_call_target="tpu_custom_call" | custom-call | tf_op jit(solution)/shard_map/write/pallas_call | solution.py:449

commit v5 on v4

--- a/solution.py
+++ b/solution.py
@@ -60,7 +60,7 @@
     def nth_head(self, n):
         step = n // 2
         far = (step + 1) // 2
-        turn = jnp.where(lax.rem(step, 2) == 1, far, 8 - far)
+        turn = jnp.where(lax.rem(step + self.core, 2) == 1, far, 8 - far)
         return 8 * lax.rem(self.head // 8 + n, 2) + lax.rem(self.head + turn, 8)
 
     def nth_tile(self, n):
@@ -88,7 +88,8 @@
             def _():
                 pl.semaphore_signal(barrier, 1, device_id=other, device_id_type=MESH)
 
-    loop(HEADS, signal)
+    for i in range(HEADS):
+        signal(jnp.int32(i))
     has_before, has_after = me.slice > 0, me.slice < me.last
 
     @pl.when(has_before)

time: 111 us -> 111 us (level)
  no operation moved by 1% of the time
where the time goes in v5:
time: 111 us; the launch traced here: 110 us
  Pallas kernels  109 us (98%)
    pallas_call x1, Pallas kernels, body(): pl.pallas_call(attention_kernel, out_shape=[rows] * 4, in_specs=[smem] *...  107 us
    pallas_call x1, Pallas kernels, body(): pl.pallas_call(write_kernel, out_shape=[rows] * 4, in_specs=[anywhere] *...  2.42 us

profile of v5, /device:TPU:35, one launch (start us, length us, event | category | flops | bytes accessed | tf_op | source)
XLA Modules:
  0.0 109.6 jit_solution(5631017337769786)
XLA Ops:
  0.6 106.5 %attention.1 = (bf16[128,2048]{1,0:T(8,128)(2,1)}, bf16[128,2048]{1,0:T(8,128)(2,1)}, bf16[128,2048]{1,0:T(8,128)(2,1)}, bf16[128,2048]{1,0:T(8,128)(2,1)}) custom-call(s32[6,128]{1,0:T(8,128)} %bitcast.2, s32[8,16]{1,0:T(8,128)} %bitcast.3, bf16[128,2048]{1,0:T(8,128)(2,1)} %q_in.1, bf16[128,2048]{1,0:T(8,128)(2,1)} %k_in.1, bf16[128,2048]{1,0:T(8,128)(2,1)} %v_in.1, ...), custom_call_target="tpu_custom_call" | custom-call | tf_op jit(solution)/shard_map/attention/pallas_call | solution.py:433
  107.1 2.4 %write.1 = (bf16[128,2048]{1,0:T(8,128)(2,1)}, bf16[128,2048]{1,0:T(8,128)(2,1)}, bf16[128,2048]{1,0:T(8,128)(2,1)}, bf16[128,2048]{1,0:T(8,128)(2,1)}) custom-call(bf16[128,2048]{1,0:T(8,128)(2,1)} %get-tuple-element.8.refs_0_, bf16[128,2048]{1,0:T(8,128)(2,1)} %get-tuple-element.9.refs_1_, bf16[128,2048]{1,0:T(8,128)(2,1)} %get-tuple-element.10.refs_2_, ...), custom_call_target="tpu_custom_call" | custom-call | tf_op jit(solution)/shard_map/write/pallas_call | solution.py:450
